TPU v7x, 256 devices: a whole 4x4x8 slice. The times are simulated.
256 devices in a mesh: dp: 16 (over z, core), seq: 16 (over y, x).
Axes of the slice: x: 4, y: 4, z: 8, core: 2. Of those that a mesh axis runs over, the one named last changes fastest.
Arguments:
- resid: bfloat16 [16, 2048, 1536], P('dp', 'seq'), may hold values from -6 to 6
- query: bfloat16 [16, 2048, 1024], P('dp', 'seq'), may hold values from -30 to 30
- key: bfloat16 [16, 2048, 1024], P('dp', 'seq'), may hold values from -30 to 30
- value: bfloat16 [16, 2048, 1024], P('dp', 'seq'), may hold values from -6 to 6
- out_weight: bfloat16 [1024, 1536], replicated, may hold values from -0.1875 to 0.1875
- conv_kernel: float32 [31, 1536], replicated, may hold values from -1 to 1
- conv_gain: float32 [1536], replicated, may hold values from 0.1 to 1.9
- recording_ids: int32 [16, 2048], P('dp', 'seq'), may hold values from 0 to 5, never falling along the last dimension, each value on 1 to 1024 neighbouring positions
- cotangent: bfloat16 [16, 2048, 1536], P('dp', 'seq'), may hold values from -6 to 6
Outputs:
- layer_out: bfloat16 [16, 2048, 1536], P('dp', 'seq')
- grad_resid: bfloat16 [16, 2048, 1536], P('dp', 'seq')
- grad_query: bfloat16 [16, 2048, 1024], P('dp', 'seq')
- grad_key: bfloat16 [16, 2048, 1024], P('dp', 'seq')
- grad_value: bfloat16 [16, 2048, 1024], P('dp', 'seq')
- grad_out_weight: float32 [1024, 1536], P(('dp', 'seq'))
- grad_kernel: float32 [31, 1536], replicated
- grad_gain: float32 [1536], replicated
Inputs may be any that keep to these rules, and one draw needn't show every extreme that they name: `recording_ids`: recording ids never fall along a sequence; each of the 6 recordings occupies 1 to 1024 consecutive frames, one of them exactly 1024.
All inputs are finite; a program needn't handle non-finite values.
Results may differ from a plain program's by a relative error of at most 0.034.
Values may be sent and summed in bfloat16 or wider, within the bound.
A program may use at most 192 MiB of HBM per device.

v0:
```python
import jax
import jax.numpy as jnp
from jax import lax
from jax.sharding import PartitionSpec as P

HEAD = 64


NEGATIVE = -1e30
EPSILON = 1e-05


def with_halo(value, sides, width):
    for axis, dim in sides:
        devices, length = (lax.axis_size(axis), value.shape[dim])
        up = [(i, (i + 1) % devices) for i in range(devices - 1)]
        down = [(j, i) for i, j in up]
        last = lax.slice_in_dim(value, length - width, length, axis=dim)
        initial = lax.slice_in_dim(value, 0, width, axis=dim)
        before = lax.ppermute(last, axis, up)
        after = lax.ppermute(initial, axis, down)
        value = jnp.concatenate([before, value, after], axis=dim)
    return value


def to_heads(rows, head_count):
    return rows.reshape(rows.shape[0], head_count, -1).transpose(1, 0, 2)


def from_heads(blocks):
    return blocks.transpose(1, 0, 2).reshape(blocks.shape[1], -1)


def attend(q_heads, k_heads, v_heads, ids_rows, ids_keys, active, scale):
    head_count, length, size = q_heads.shape
    blocks = length // length
    q_blocks = q_heads.reshape(head_count, blocks, length, size).swapaxes(0, 1)
    id_blocks = ids_rows.reshape(blocks, length)
    act_blocks = active.reshape(blocks, length)

    def compute(inputs):
        q_part, id_part, act_part = inputs
        matches = (id_part[:, None] == ids_keys[None, :]) & act_part[:, None]
        scores = (
            jnp.einsum("hae,hbe->hab", q_part, k_heads, preferred_element_type=jnp.float32) * scale
        )
        scores = jnp.where(matches[None], scores, NEGATIVE)
        row_max = jnp.max(scores, axis=-1)
        unnormed = jnp.where(matches[None], jnp.exp(scores - row_max[..., None]), 0.0)
        row_sum = jnp.where(act_part[None], jnp.sum(unnormed, axis=-1), 1.0)
        row_max = jnp.where(act_part[None], row_max, 0.0)
        weights = (unnormed / row_sum[..., None]).astype(jnp.bfloat16)
        result = jnp.einsum(
            "hab,hbe->hae", weights, v_heads, preferred_element_type=jnp.float32
        ).astype(jnp.bfloat16)
        return (result, row_max, row_sum)

    def bypass(inputs):
        q_part = inputs[0]
        return (
            jnp.zeros(q_part.shape, jnp.bfloat16),
            jnp.zeros(q_part.shape[:2], jnp.float32),
            jnp.ones(q_part.shape[:2], jnp.float32),
        )

    def one_block(inputs):
        return lax.cond(jnp.any(inputs[2]), compute, bypass, inputs)

    result, row_max, row_sum = lax.map(one_block, (q_blocks, id_blocks, act_blocks))
    result = result.swapaxes(0, 1).reshape(head_count, length, size)
    row_max = row_max.swapaxes(0, 1).reshape(head_count, length)
    row_sum = row_sum.swapaxes(0, 1).reshape(head_count, length)
    return (result, row_max, row_sum)


def backward_block(
    q_part,
    grad_part,
    row_max,
    row_sum,
    row_dot,
    k_heads,
    v_heads,
    matches,
    scale,
    want_queries,
    want_keys,
):
    scores = jnp.einsum("hae,hbe->hab", q_part, k_heads, preferred_element_type=jnp.float32) * scale
    unnormed = jnp.where(matches[None], jnp.exp(scores - row_max[..., None]), 0.0)
    weights = (unnormed / row_sum[..., None]).astype(jnp.bfloat16)
    drift = jnp.einsum("hae,hbe->hab", grad_part, v_heads, preferred_element_type=jnp.float32)
    slope = (weights.astype(jnp.float32) * (drift - row_dot[..., None])).astype(jnp.bfloat16)
    grad_q = None
    grad_k = None
    grad_v = None
    if want_queries:
        grad_q = jnp.einsum("hab,hbe->hae", slope, k_heads, preferred_element_type=jnp.float32)
    if want_keys:
        grad_k = jnp.einsum("hab,hae->hbe", slope, q_part, preferred_element_type=jnp.float32)
        grad_v = jnp.einsum("hab,hae->hbe", weights, grad_part, preferred_element_type=jnp.float32)
    return (grad_q, grad_k, grad_v)


def local(resid, query, key, value, out_weight, conv_kernel, conv_gain, recording_ids, cotangent):
    frames = resid.shape[1]
    attn_width = query.shape[2]
    head_count = attn_width // HEAD
    scale = HEAD ** (-0.5)
    taps = conv_kernel.shape[0]
    margin = taps // 2
    all_ids = lax.all_gather(recording_ids[0], "seq", axis=0, tiled=True)
    offset = lax.axis_index("seq") * frames
    own_ids = lax.dynamic_slice_in_dim(all_ids, offset, frames)
    q_rows = query[0]
    k_rows = key[0]
    v_rows = value[0]
    k_all, v_all = (
        lax.all_gather(k_rows, "seq", axis=0, tiled=True),
        lax.all_gather(v_rows, "seq", axis=0, tiled=True),
    )
    q_heads = to_heads(q_rows, head_count)
    k_heads = to_heads(k_all, head_count)
    v_heads = to_heads(v_all, head_count)
    out_heads, row_max, row_sum = attend(
        q_heads, k_heads, v_heads, own_ids, all_ids, jnp.ones((frames,), jnp.bool_), scale
    )
    attn = from_heads(out_heads)
    stream = resid[0].astype(jnp.float32) + jnp.dot(
        attn, out_weight, preferred_element_type=jnp.float32
    )
    norm_factor = lax.rsqrt(jnp.mean(stream * stream, axis=-1, keepdims=True) + EPSILON)
    normed = stream * norm_factor
    shaped = (normed * conv_gain).astype(jnp.bfloat16)
    shaped_pad = with_halo(shaped, (("seq", 0),), margin)
    ids_pad = jnp.pad(all_ids, (margin, margin), constant_values=-1)
    window = lax.dynamic_slice_in_dim(ids_pad, offset, frames + 2 * margin)
    conv = jnp.zeros(stream.shape, jnp.float32)
    for position in range(taps):
        match_fore = (window[position : position + frames] == own_ids)[:, None]
        conv = conv + jnp.where(
            match_fore, conv_kernel[position] * shaped_pad[position : position + frames], 0.0
        )
    layer_out = (stream + jax.nn.silu(conv)).astype(jnp.bfloat16)
    sigma = jax.nn.sigmoid(conv)
    grad_conv = (cotangent[0].astype(jnp.float32) * sigma * (1.0 + conv * (1.0 - sigma))).astype(
        jnp.bfloat16
    )
    grad_pad = with_halo(grad_conv, (("seq", 0),), margin)
    grad_shaped = jnp.zeros(stream.shape, jnp.float32)
    kernel_rows = []
    for position in range(taps):
        mirror = 2 * margin - position
        match_back = (window[mirror : mirror + frames] == own_ids)[:, None]
        grad_shaped = grad_shaped + jnp.where(
            match_back, conv_kernel[position] * grad_pad[mirror : mirror + frames], 0.0
        )
        match_fore = (window[position : position + frames] == own_ids)[:, None]
        kernel_rows.append(
            jnp.sum(
                jnp.where(
                    match_fore,
                    grad_conv.astype(jnp.float32)
                    * shaped_pad[position : position + frames].astype(jnp.float32),
                    0.0,
                ),
                axis=0,
            )
        )
    kernel_part = jnp.stack(kernel_rows)
    gain_part = jnp.sum(grad_shaped * normed, axis=0)
    kernel_sum, gain_sum = lax.psum((kernel_part, gain_part), ("dp", "seq"))
    scaled = grad_shaped * conv_gain
    grad_stream = cotangent[0].astype(jnp.float32) + norm_factor * (
        scaled - normed * jnp.mean(scaled * normed, axis=-1, keepdims=True)
    )
    grad_resid = grad_stream.astype(jnp.bfloat16)
    grad_attn = lax.dot_general(
        grad_resid, out_weight, (((1,), (1,)), ((), ())), preferred_element_type=jnp.float32
    ).astype(jnp.bfloat16)
    weight_grad = lax.psum_scatter(
        lax.dot_general(
            attn, grad_resid, (((0,), (0,)), ((), ())), preferred_element_type=jnp.float32
        ),
        ("dp", "seq"),
        scatter_dimension=0,
        tiled=True,
    )
    grad_heads = to_heads(grad_attn, head_count)
    row_dot = jnp.sum(grad_heads.astype(jnp.float32) * out_heads.astype(jnp.float32), axis=-1)
    own_matches = own_ids[:, None] == all_ids[None, :]
    local_grads = backward_block(
        q_heads,
        grad_heads,
        row_max,
        row_sum,
        row_dot,
        k_heads,
        v_heads,
        own_matches,
        scale,
        True,
        False,
    )
    grad_query = from_heads((local_grads[0] * scale).astype(jnp.bfloat16))
    max_all, sum_all, dot_all = (
        lax.all_gather(row_max, "seq", axis=1, tiled=True),
        lax.all_gather(row_sum, "seq", axis=1, tiled=True),
        lax.all_gather(row_dot, "seq", axis=1, tiled=True),
    )
    k_local = to_heads(k_rows, head_count)
    v_local = to_heads(v_rows, head_count)
    q_piece = lax.all_gather(q_rows, "seq", axis=0, tiled=True)
    grad_piece = lax.all_gather(grad_attn, "seq", axis=0, tiled=True)
    matches = all_ids[:, None] == own_ids[None, :]
    grads = backward_block(
        to_heads(q_piece, head_count),
        to_heads(grad_piece, head_count),
        max_all,
        sum_all,
        dot_all,
        k_local,
        v_local,
        matches,
        scale,
        False,
        True,
    )
    grad_key = from_heads((grads[1] * scale).astype(jnp.bfloat16))
    grad_value = from_heads(grads[2].astype(jnp.bfloat16))
    return (
        layer_out[None],
        grad_resid[None],
        grad_query[None],
        grad_key[None],
        grad_value[None],
        weight_grad,
        kernel_sum,
        gain_sum,
    )


def solution(mesh):
    placed = (
        P("dp", "seq", None),
        P("dp", "seq", None),
        P("dp", "seq", None),
        P("dp", "seq", None),
        P(),
        P(),
        P(),
        P("dp", "seq"),
        P("dp", "seq", None),
    )
    return jax.shard_map(
        local,
        mesh=mesh,
        in_specs=placed,
        out_specs=(
            P("dp", "seq", None),
            P("dp", "seq", None),
            P("dp", "seq", None),
            P("dp", "seq", None),
            P("dp", "seq", None),
            P(("dp", "seq"), None),
            P(),
            P(),
        ),
        check_vma=False,
    )
```

profile of v0, /device:TPU:8, one launch (start us, length us, event | category | flops | bytes accessed | tf_op | source)
XLA Modules:
  0.0 596.2 jit_solution(3103317406553935389)
XLA Ops:
  9.5 1.8 copy.38
  11.2 20.5 %all-gather = s32[1,2048]{1,0:T(1,128)S(1)} all-gather(s32[1,128]{1,0:T(1,128)} %param.16), channel_id=2, replica_groups=mesh['dp'=16,'seq'=16] {'seq'}, dimensions={1}, use_global_device_ids=true | all-gather | bytes 8704 | tf_op jit(solution)/shard_map/all_gather | solution.py:112
  34.0 2.5 slice_reduce_fusion.30
  36.5 33.4 %all-gather.11.cloned.1.call-done = bf16[1,2048,1024]{2,1,0:T(8,128)(2,1)} async-done(((bf16[1,128,1024]{2,1,0:T(8,128)(2,1)}), bf16[1,2048,1024]{2,1,0:T(8,128)(2,1)}) %all-gather.11.cloned.1.call-update) | async-done | bytes 4194320 | tf_op jit(solution)/shard_map/all_gather | solution.py:119
  69.9 6.5 %copy.39 = bf16[1,2048,1024]{1,2,0:T(8,128)(2,1)} copy(bf16[1,2048,1024]{2,1,0:T(8,128)(2,1)} %all-gather.11.cloned.1.call-done) | data formatting | bytes 8388608 | tf_op jit(solution)/shard_map/all_gather | solution.py:119
  76.4 4.9 select_reduce_fusion
  81.3 5.8 copy-done.2
  87.1 5.0 fusion
  92.1 36.5 %all-gather.13.cloned.1.call-done = bf16[1,2048,1024]{2,1,0:T(8,128)(2,1)} async-done(((bf16[1,128,1024]{2,1,0:T(8,128)(2,1)}), bf16[1,2048,1024]{2,1,0:T(8,128)(2,1)}) %all-gather.13.cloned.1.call-update) | async-done | bytes 4194320 | tf_op jit(solution)/shard_map/all_gather | solution.py:120
  128.6 6.5 %copy.40 = bf16[1,2048,1024]{1,2,0:T(8,128)(2,1)} copy(bf16[1,2048,1024]{2,1,0:T(8,128)(2,1)} %all-gather.13.cloned.1.call-done) | data formatting | bytes 8388608 | tf_op jit(solution)/shard_map/all_gather | solution.py:120
  135.5 9.6 %fusion.13 = bf16[16,128,64]{1,2,0:T(8,128)(2,1)S(1)} fusion(bf16[16,2048,64]{1,2,0:T(8,128)(2,1)} %bitcast.75, f32[16,128,2048]{2,1,0:T(8,128)} %copy-done.2, f32[16,128]{1,0:T(8,128)S(1)} %fusion, f32[16,128]{1,0:T(8,128)S(1)} %get-tuple-element.178, pred[128,2048]{1,0:T(8,128)(4,1)S(1)} %broadcast_compare_fusion.1), kind=kOutput, calls=%fused_computation.109 | convolution fusion | flops 562167808 | bytes 21512192 | tf_op jit(solution)/shard_map/while/body/eval_jaxpr/cond/branch_1_fun/hab,hbe->hae/dot_general | solution.py:53
  146.1 4.6 collective-permute-start.1
  150.7 2.4 collective-permute-start
  153.1 1.5 slice_reduce_fusion.29
  154.8 4.1 collective-permute-done
  159.2 12.8 %fusion.154 = (f32[1536]{0:T(1024)S(1)}, f32[1536]{0:T(1024)S(1)}, f32[1536]{0:T(1024)S(1)}, f32[1536]{0:T(1024)S(1)}, f32[1536]{0:T(1024)S(1)}, /*index=5*/f32[...) fusion(pred[128]{0:T(512)(128)(4,1)} %get-tuple-element.150, ...), kind=kLoop, calls=%fused_computation.283 | loop fusion | flops 52288512 | bytes 2289536 | tf_op jit(solution)/shard_map/reduce_sum | solution.py:160
  172.7 1.9 collective-permute-start.3
  174.6 6.0 %collective-permute-start.2 = (bf16[15,1536]{1,0:T(8,128)(2,1)}, bf16[15,1536]{1,0:T(8,128)(2,1)}, u32[]{:S(2)}, u32[]{:S(2)}) collective-permute-start(bf16[15,1536]{1,0:T(8,128)(2,1)} %get-tuple-element.144), channel_id=1, source_target_pairs={{1,0},{2,1},{3,2},{4,3},{5,4},{6,5},{7,6},{8,7},{9,8},{10,9},{11,1... | collective-permute-start | bytes 138248 | tf_op jit(solution)/shard_map/ppermute | solution.py:21
  180.6 1.3 fusion.152
  181.9 2.2 fusion.124
  184.1 2.7 fusion.156
  186.8 1.4 fusion.122
  188.2 1.1 fusion.102
  207.8 6.0 stack.127
  213.8 8.3 %multiply_reduce_fusion = (f32[1536]{0:T(1024)}, f32[128]{0:T(128)S(1)}, f32[128,1536]{1,0:T(8,128)S(1)}) fusion(f32[128,1536]{1,0:T(8,128)} %copy-done.3, f32[128]{0:T(128)} %copy-done.65, f32[1536]{0:T(1024)} %param.15, bf16[128,1536]{1,0:T(8,128)(2,1)S(1)} %get-tuple-element.137, bf16[15,1536]{1,0:T(8,128)(2,1)} %collective-permute-done.3, ...), kind=kLoop, calls=%fused_computation.286 | loop fusion | flops 43055488 | bytes 2265984 | tf_op jit(solution)/shard_map/reduce_sum | solution.py:171
  222.1 2.7 fusion.77
  224.8 4.8 fusion.224
  229.8 1.8 convolution_convert_fusion.1
  231.6 1.1 copy.43
  232.8 1.8 copy.45
  234.6 1.0 broadcast_compare_fusion
  235.6 6.6 %copy.42 = bf16[1,2048,1024]{1,2,0:T(8,128)(2,1)} copy(bf16[1,2048,1024]{2,1,0:T(8,128)(2,1)} %all-gather.15.cloned.1.call-done) | data formatting | bytes 8388608 | tf_op jit(solution)/shard_map/all_gather | solution.py:213
  242.1 20.3 %all_gather.29 = f32[16,2048]{1,0:T(8,128)S(1)} all-gather(f32[16,128]{1,0:T(8,128)S(1)} %copy-done.45), channel_id=1, replica_groups=mesh['dp'=16,'seq'=16] {'seq'}, dimensions={1}, use_global_device_ids=true | all-gather | bytes 139264 | tf_op jit(solution)/shard_map/all_gather | solution.py:208
  262.5 23.3 %all_gather.28 = f32[16,2048]{1,0:T(8,128)S(1)} all-gather(f32[16,128]{1,0:T(8,128)S(1)} %get-tuple-element.178), channel_id=1, replica_groups=mesh['dp'=16,'seq'=16] {'seq'}, dimensions={1}, use_global_device_ids=true | all-gather | bytes 139264 | tf_op jit(solution)/shard_map/all_gather | solution.py:207
  285.8 14.0 %divide_convert_fusion = bf16[16,2048,128]{2,1,0:T(8,128)(2,1)} fusion(f32[16,2048]{1,0:T(8,128)S(1)} %all_gather.29, f32[16,2048]{1,0:T(8,128)S(1)} %all_gather.28, pred[2048,128]{1,0:T(8,128)(4,1)S(1)} %broadcast_compare_fusion, bf16[16,2048,64]{1,2,0:T(8,128)(2,1)} %bitcast.77, bf16[16,128,64]{1,2,0:T(8,128)(2,1)S(1)} %bitcast.86), kind=kOutput, calls=%fused_computation.1 | convolution fusion | flops 557842432 | bytes 13369344 | tf_op jit(solution)/shard_map/hae,hbe->hab/dot_general | solution.py:89
  300.1 12.9 %fusion.12 = bf16[16,128,64]{1,2,0:T(8,128)(2,1)S(1)} fusion(bf16[16,2048,64]{1,2,0:T(8,128)(2,1)} %bitcast.74, f32[16,128,2048]{2,1,0:T(8,128)} %copy-done.2, f32[16,128]{1,0:T(8,128)S(1)} %multiply_reduce_fusion.3, f32[16,128]{1,0:T(8,128)S(1)} %copy-done.45, f32[16,128]{1,0:T(8,128)S(1)} %get-tuple-element.178, pred[128,2048]{1,0:T(8,128)(4,1)S(1)} %copy-done.8, ...), kind=kOutput, calls=%fused_computation.108 | convolution fusion | flops 1111752704 | bytes 25976832 | tf_op jit(solution)/shard_map/hab,hbe->hae/dot_general | solution.py:98
  313.0 0.8 copy.46
  313.8 74.1 %psum.15 = f32[1536]{0:T(1024)} all-reduce(f32[1536]{0:T(1024)S(1)} %copy-done.46), channel_id=1, replica_groups=mesh['dp'=16,'seq'=16] {'dp','seq'}, use_global_device_ids=true, to_apply=%region_39.40 | all-reduce | flops 1536 | bytes 12288 | tf_op jit(solution)/shard_map/psum | solution.py:172
  387.9 24.0 %all_gather.31 = f32[16,2048]{1,0:T(8,128)S(1)} all-gather(f32[16,128]{1,0:T(8,128)S(1)} %multiply_reduce_fusion.3), channel_id=1, replica_groups=mesh['dp'=16,'seq'=16] {'seq'}, dimensions={1}, use_global_device_ids=true | all-gather | bytes 139264 | tf_op jit(solution)/shard_map/all_gather | solution.py:209
  411.9 90.8 %all-reduce.5.cloned.1.call-done = (f32[1024,1536]{1,0:T(8,128)}, f32[31,1536]{1,0:T(8,128)}) async-done(((f32[1024,1536]{1,0:T(8,128)}, f32[31,1536]{1,0:T(8,128)}), (f32[1024,1536]{1,0:T(8,128)}, f32[31,1536]{1,0:T(8,128)})) %all-reduce.5.cloned.1.call-update) | async-done | bytes 6481936
  502.7 1.4 constant_dynamic-slice_fusion
  504.1 56.7 %all-gather.9.cloned.1.call-done = bf16[2048,1024]{1,0:T(8,128)(2,1)} async-done(((bf16[128,1024]{1,0:T(8,128)(2,1)}), bf16[2048,1024]{1,0:T(8,128)(2,1)}) %all-gather.9.cloned.1.call-update) | async-done | bytes 4194320 | tf_op jit(solution)/shard_map/all_gather | solution.py:214
  560.8 6.5 %copy.44 = bf16[2048,1024]{0,1:T(8,128)(2,1)} copy(bf16[2048,1024]{1,0:T(8,128)(2,1)} %all-gather.9.cloned.1.call-done) | data formatting | bytes 8388608 | tf_op jit(solution)/shard_map/all_gather | solution.py:214
  567.3 6.2 %convolution_convert_fusion = bf16[16,128,64]{1,2,0:T(8,128)(2,1)S(1)} fusion(bf16[16,2048,64]{1,2,0:T(8,128)(2,1)} %bitcast.71, bf16[16,2048,128]{2,1,0:T(8,128)(2,1)} %divide_convert_fusion), kind=kOutput, calls=%fused_computation.106 | convolution fusion | flops 537001984 | bytes 12845056 | tf_op jit(solution)/shard_map/hab,hae->hbe/dot_general | solution.py:101
  573.5 11.7 %fusion.11 = bf16[16,128,64]{1,2,0:T(8,128)(2,1)} fusion(bf16[16,2048,64]{1,2,0:T(8,128)(2,1)} %bitcast.78, bf16[16,2048,128]{2,1,0:T(8,128)(2,1)} %divide_convert_fusion, f32[16,2048]{1,0:T(8,128)S(1)} %all_gather.31, bf16[16,2048,64]{1,2,0:T(8,128)(2,1)} %bitcast.72, bf16[16,128,64]{1,2,0:T(8,128)(2,1)} %bitcast.85), kind=kOutput, calls=%fused_computation.105 | convolution fusion | flops 1090781184 | bytes 17432576 | tf_op jit(solution)/shard_map/hab,hae->hbe/dot_general | solution.py:100
  585.2 1.8 copy.47
  587.0 0.8 copy.48
  587.9 1.6 copy.51
  (189 shorter events, 25.3 us)
Async XLA Ops:
  7.2 138.0 %copy-start = (bf16[1024,1536]{1,0:T(8,128)(2,1)S(1)}, bf16[1024,1536]{1,0:T(8,128)(2,1)}, u32[]{:S(2)}) copy-start(bf16[1024,1536]{1,0:T(8,128)(2,1)} %param.13) | copy-start | bytes 9437188
  7.2 62.7 %all-gather.11.cloned.1.call-start = ((), (), s32[]{:S(2)}) async-start(), calls=%async_computation.1 | async-start | bytes 4456448 | tf_op jit(solution)/shard_map/all_gather | solution.py:119
  7.9 120.7 %all-gather.13.cloned.1.call-start = ((), (), s32[]{:S(2)}) async-start(), calls=%async_computation.2 | async-start | bytes 4456448 | tf_op jit(solution)/shard_map/all_gather | solution.py:120
  8.7 226.9 %all-gather.15.cloned.1.call-start = ((), (), s32[]{:S(2)}) async-start(), calls=%async_computation.3 | async-start | bytes 4456448 | tf_op jit(solution)/shard_map/all_gather | solution.py:213
  9.4 493.3 %all-reduce.5.cloned.1.call-start = ((), (), s32[]{:S(2)}) async-start(), calls=%async_computation.4 | async-start | bytes 12976128
  32.3 49.0 %copy-start.47 = (s32[128]{0:T(128)}, s32[128]{0:T(128)S(1)}, u32[]{:S(2)}) copy-start(s32[128]{0:T(128)S(1)} %get-tuple-element.141) | copy-start | bytes 1540
  32.6 102.6 %copy-start.7 = (pred[128,2048]{1,0:T(8,128)(4,1)}, pred[128,2048]{1,0:T(8,128)(4,1)S(1)}, u32[]{:S(2)}) copy-start(pred[128,2048]{1,0:T(8,128)(4,1)S(1)} %broadcast_compare_fusion.1) | copy-start | bytes 786436
  92.1 53.1 %copy-start.44 = (f32[16,128]{1,0:T(8,128)}, f32[16,128]{1,0:T(8,128)S(1)}, u32[]{:S(2)}) copy-start(f32[16,128]{1,0:T(8,128)S(1)} %fusion) | copy-start | bytes 24580
  135.1 23.7 %copy-start.10 = (bf16[1,128,1536]{2,1,0:T(8,128)(2,1)S(1)}, bf16[1,128,1536]{2,1,0:T(8,128)(2,1)}, u32[]{:S(2)}) copy-start(bf16[1,128,1536]{2,1,0:T(8,128)(2,1)} %param.17) | copy-start | bytes 1179652
  135.1 23.7 %copy-start.13 = (f32[1536]{0:T(1024)S(1)}, f32[1536]{0:T(1024)}, u32[]{:S(2)}) copy-start(f32[1536]{0:T(1024)} %get-tuple-element.104) | copy-start | bytes 18436
  135.2 23.7 %copy-start.14 = (f32[1536]{0:T(1024)S(1)}, f32[1536]{0:T(1024)}, u32[]{:S(2)}) copy-start(f32[1536]{0:T(1024)} %get-tuple-element.105) | copy-start | bytes 18436
  135.2 23.7 %copy-start.15 = (f32[1536]{0:T(1024)S(1)}, f32[1536]{0:T(1024)}, u32[]{:S(2)}) copy-start(f32[1536]{0:T(1024)} %get-tuple-element.106) | copy-start | bytes 18436
  135.2 23.7 %copy-start.16 = (f32[1536]{0:T(1024)S(1)}, f32[1536]{0:T(1024)}, u32[]{:S(2)}) copy-start(f32[1536]{0:T(1024)} %get-tuple-element.107) | copy-start | bytes 18436
  135.2 23.7 %copy-start.17 = (f32[1536]{0:T(1024)S(1)}, f32[1536]{0:T(1024)}, u32[]{:S(2)}) copy-start(f32[1536]{0:T(1024)} %get-tuple-element.108) | copy-start | bytes 18436
  135.2 23.7 %copy-start.18 = (f32[1536]{0:T(1024)S(1)}, f32[1536]{0:T(1024)}, u32[]{:S(2)}) copy-start(f32[1536]{0:T(1024)} %get-tuple-element.109) | copy-start | bytes 18436
  135.2 23.7 %copy-start.19 = (f32[1536]{0:T(1024)S(1)}, f32[1536]{0:T(1024)}, u32[]{:S(2)}) copy-start(f32[1536]{0:T(1024)} %get-tuple-element.110) | copy-start | bytes 18436
  135.2 23.7 %copy-start.20 = (f32[1536]{0:T(1024)S(1)}, f32[1536]{0:T(1024)}, u32[]{:S(2)}) copy-start(f32[1536]{0:T(1024)} %get-tuple-element.111) | copy-start | bytes 18436
  135.2 23.7 %copy-start.21 = (f32[1536]{0:T(1024)S(1)}, f32[1536]{0:T(1024)}, u32[]{:S(2)}) copy-start(f32[1536]{0:T(1024)} %get-tuple-element.112) | copy-start | bytes 18436
  135.2 23.7 %copy-start.22 = (f32[1536]{0:T(1024)S(1)}, f32[1536]{0:T(1024)}, u32[]{:S(2)}) copy-start(f32[1536]{0:T(1024)} %get-tuple-element.113) | copy-start | bytes 18436
  135.2 23.7 %copy-start.23 = (f32[1536]{0:T(1024)S(1)}, f32[1536]{0:T(1024)}, u32[]{:S(2)}) copy-start(f32[1536]{0:T(1024)} %get-tuple-element.114) | copy-start | bytes 18436
  135.3 23.7 %copy-start.24 = (f32[1536]{0:T(1024)S(1)}, f32[1536]{0:T(1024)}, u32[]{:S(2)}) copy-start(f32[1536]{0:T(1024)} %get-tuple-element.115) | copy-start | bytes 18436
  135.3 23.7 %copy-start.25 = (f32[1536]{0:T(1024)S(1)}, f32[1536]{0:T(1024)}, u32[]{:S(2)}) copy-start(f32[1536]{0:T(1024)} %get-tuple-element.116) | copy-start | bytes 18436
  135.3 23.7 %copy-start.26 = (f32[1536]{0:T(1024)S(1)}, f32[1536]{0:T(1024)}, u32[]{:S(2)}) copy-start(f32[1536]{0:T(1024)} %get-tuple-element.117) | copy-start | bytes 18436
  135.3 23.7 %copy-start.27 = (f32[1536]{0:T(1024)S(1)}, f32[1536]{0:T(1024)}, u32[]{:S(2)}) copy-start(f32[1536]{0:T(1024)} %get-tuple-element.118) | copy-start | bytes 18436
  135.3 23.7 %copy-start.28 = (f32[1536]{0:T(1024)S(1)}, f32[1536]{0:T(1024)}, u32[]{:S(2)}) copy-start(f32[1536]{0:T(1024)} %get-tuple-element.119) | copy-start | bytes 18436
  135.3 23.7 %copy-start.29 = (f32[1536]{0:T(1024)S(1)}, f32[1536]{0:T(1024)}, u32[]{:S(2)}) copy-start(f32[1536]{0:T(1024)} %get-tuple-element.120) | copy-start | bytes 18436
  135.3 23.7 %copy-start.30 = (f32[1536]{0:T(1024)S(1)}, f32[1536]{0:T(1024)}, u32[]{:S(2)}) copy-start(f32[1536]{0:T(1024)} %get-tuple-element.121) | copy-start | bytes 18436
  135.3 23.7 %copy-start.31 = (f32[1536]{0:T(1024)S(1)}, f32[1536]{0:T(1024)}, u32[]{:S(2)}) copy-start(f32[1536]{0:T(1024)} %get-tuple-element.122) | copy-start | bytes 18436
  135.3 23.7 %copy-start.48 = (pred[128]{0:T(512)(128)(4,1)S(1)}, pred[128]{0:T(512)(128)(4,1)}, u32[]{:S(2)}) copy-start(pred[128]{0:T(512)(128)(4,1)} %get-tuple-element.140) | copy-start | bytes 388
  135.3 23.7 %copy-start.49 = (pred[128]{0:T(512)(128)(4,1)S(1)}, pred[128]{0:T(512)(128)(4,1)}, u32[]{:S(2)}) copy-start(pred[128]{0:T(512)(128)(4,1)} %get-tuple-element.148) | copy-start | bytes 388
  145.2 44.1 %copy-start.4 = (bf16[16,128,64]{1,2,0:T(8,128)(2,1)}, bf16[16,128,64]{1,2,0:T(8,128)(2,1)S(1)}, u32[]{:S(2)}) copy-start(bf16[16,128,64]{1,2,0:T(8,128)(2,1)S(1)} %fusion.13) | copy-start | bytes 786436
  146.1 8.7 %collective-permute-start.1 = (bf16[15,1536]{1,0:T(8,128)(2,1)S(1)}, bf16[15,1536]{1,0:T(8,128)(2,1)S(1)}, u32[]{:S(2)}, u32[]{:S(2)}) collective-permute-start(bf16[15,1536]{1,0:T(8,128)(2,1)S(1)} %get-tuple-element.147), channel_id=1, source_target_pairs={{1,0},{2,1},{3,2},{4,3},{5,4},{6,5},{7,6},{8,7},{9,8},{10,9},{11,1... | collective-permute-start | bytes 138248 | tf_op jit(solution)/shard_map/ppermute | solution.py:21
  150.7 8.1 %collective-permute-start = (bf16[15,1536]{1,0:T(8,128)(2,1)S(1)}, bf16[15,1536]{1,0:T(8,128)(2,1)S(1)}, u32[]{:S(2)}, u32[]{:S(2)}) collective-permute-start(bf16[15,1536]{1,0:T(8,128)(2,1)S(1)} %get-tuple-element.146), channel_id=1, source_target_pairs={{0,1},{1,2},{2,3},{3,4},{4,5},{5,6},{6,7},{7,8},{8,9},{9,10},{10,1... | collective-permute-start | bytes 138248 | tf_op jit(solution)/shard_map/ppermute | solution.py:20
  154.6 34.7 %copy-start.32 = (f32[1536]{0:T(1024)}, f32[1536]{0:T(1024)S(1)}, u32[]{:S(2)}) copy-start(f32[1536]{0:T(1024)S(1)} %get-tuple-element.123) | copy-start | bytes 18436
  154.6 35.3 %copy-start.33 = (f32[1536]{0:T(1024)}, f32[1536]{0:T(1024)S(1)}, u32[]{:S(2)}) copy-start(f32[1536]{0:T(1024)S(1)} %get-tuple-element.124) | copy-start | bytes 18436
  154.7 35.3 %copy-start.34 = (f32[1536]{0:T(1024)}, f32[1536]{0:T(1024)S(1)}, u32[]{:S(2)}) copy-start(f32[1536]{0:T(1024)S(1)} %get-tuple-element.125) | copy-start | bytes 18436
  154.7 35.9 %copy-start.35 = (f32[1536]{0:T(1024)}, f32[1536]{0:T(1024)S(1)}, u32[]{:S(2)}) copy-start(f32[1536]{0:T(1024)S(1)} %get-tuple-element.126) | copy-start | bytes 18436
  154.7 35.9 %copy-start.36 = (f32[1536]{0:T(1024)}, f32[1536]{0:T(1024)S(1)}, u32[]{:S(2)}) copy-start(f32[1536]{0:T(1024)S(1)} %get-tuple-element.127) | copy-start | bytes 18436
  154.7 36.5 %copy-start.37 = (f32[1536]{0:T(1024)}, f32[1536]{0:T(1024)S(1)}, u32[]{:S(2)}) copy-start(f32[1536]{0:T(1024)S(1)} %get-tuple-element.128) | copy-start | bytes 18436
  154.7 36.4 %copy-start.38 = (f32[1536]{0:T(1024)}, f32[1536]{0:T(1024)S(1)}, u32[]{:S(2)}) copy-start(f32[1536]{0:T(1024)S(1)} %get-tuple-element.129) | copy-start | bytes 18436
  154.7 37.0 %copy-start.39 = (f32[1536]{0:T(1024)}, f32[1536]{0:T(1024)S(1)}, u32[]{:S(2)}) copy-start(f32[1536]{0:T(1024)S(1)} %get-tuple-element.130) | copy-start | bytes 18436
  154.7 37.0 %copy-start.40 = (f32[1536]{0:T(1024)}, f32[1536]{0:T(1024)S(1)}, u32[]{:S(2)}) copy-start(f32[1536]{0:T(1024)S(1)} %get-tuple-element.131) | copy-start | bytes 18436
  154.7 37.6 %copy-start.41 = (f32[1536]{0:T(1024)}, f32[1536]{0:T(1024)S(1)}, u32[]{:S(2)}) copy-start(f32[1536]{0:T(1024)S(1)} %get-tuple-element.132) | copy-start | bytes 18436
  154.7 37.6 %copy-start.42 = (f32[1536]{0:T(1024)}, f32[1536]{0:T(1024)S(1)}, u32[]{:S(2)}) copy-start(f32[1536]{0:T(1024)S(1)} %get-tuple-element.133) | copy-start | bytes 18436
  154.7 38.2 %copy-start.43 = (f32[1536]{0:T(1024)}, f32[1536]{0:T(1024)S(1)}, u32[]{:S(2)}) copy-start(f32[1536]{0:T(1024)S(1)} %get-tuple-element.134) | copy-start | bytes 18436
  172.7 41.1 %collective-permute-start.3 = (bf16[15,1536]{1,0:T(8,128)(2,1)}, bf16[15,1536]{1,0:T(8,128)(2,1)}, u32[]{:S(2)}, u32[]{:S(2)}) collective-permute-start(bf16[15,1536]{1,0:T(8,128)(2,1)} %get-tuple-element.145), channel_id=1, source_target_pairs={{0,1},{1,2},{2,3},{3,4},{4,5},{5,6},{6,7},{7,8},{8,9},{9,10},{10,1... | collective-permute-start | bytes 138248 | tf_op jit(solution)/shard_map/ppermute | solution.py:20
  174.6 39.2 %collective-permute-start.2 = (bf16[15,1536]{1,0:T(8,128)(2,1)}, bf16[15,1536]{1,0:T(8,128)(2,1)}, u32[]{:S(2)}, u32[]{:S(2)}) collective-permute-start(bf16[15,1536]{1,0:T(8,128)(2,1)} %get-tuple-element.144), channel_id=1, source_target_pairs={{1,0},{2,1},{3,2},{4,3},{5,4},{6,5},{7,6},{8,7},{9,8},{10,9},{11,1... | collective-permute-start | bytes 138248 | tf_op jit(solution)/shard_map/ppermute | solution.py:21
  229.5 331.3 %all-gather.9.cloned.1.call-start = ((), (), s32[]{:S(2)}) async-start(), calls=%async_computation | async-start | bytes 4456448 | tf_op jit(solution)/shard_map/all_gather | solution.py:214
  (27 other events, 495.7 us)
Sparse Core Ops, SparseCore 0:
  10.4 59.3 all-gather.10
  72.3 56.2 all-gather.12
  131.0 58.3 all-gather.14
  229.7 272.9 all-reduce.4
  505.5 55.2 all-gather.8
where the time goes:
time: 605 us; the launch traced here: 596 us
  waiting for transfers between devices  224 us (37%)
  blocking collectives  162 us (27%)
  local copies, waits for them, and re-layouts  72.7 us (12%)
  matrix products  66.7 us (11%)
  other arithmetic  40.8 us (7%)
  starting transfers between devices  15.3 us (3%)
  between operations  15.1 us (2%)
    unnamed x6, waiting for transfers between devices  92.8 us
    psum x1, blocking collectives, local(): kernel_sum, gain_sum = lax.psum((kernel_part, gain_part), ('dp', 'seq'))  74.1 us
    all_gather x1, waiting for transfers between devices, local(): grad_piece = lax.all_gather(grad_attn, 'seq', axis=0, tiled=True)  56.7 us
    all_gather x1, waiting for transfers between devices, local(): lax.all_gather(v_rows, 'seq', axis=0, tiled=True)  36.5 us
    all_gather x1, waiting for transfers between devices, local(): lax.all_gather(k_rows, 'seq', axis=0, tiled=True)  33.4 us
    another operation x32, local copies, waits for them, and re-layouts, local(): kernel_part = jnp.stack(kernel_rows)  24.4 us
    all_gather x1, blocking collectives, local(): lax.all_gather(row_dot, 'seq', axis=1, tiled=True)  24 us
    all_gather x1, blocking collectives, local(): lax.all_gather(row_max, 'seq', axis=1, tiled=True)  23.3 us
  transfers between devices with their start and end apart: 9, of which 5 were waited for; matrix products, arithmetic and copies ran while one was open for 24% of the time, Pallas kernels for 0%

commit v1 on v0

v1 whole, which is shorter than its diff:
```python
import jax
import jax.numpy as jnp
from jax import lax
from jax.experimental import pallas as pl
from jax.experimental.pallas import tpu as pltpu
from jax.sharding import PartitionSpec as P

EPSILON = 1e-05
N = 16
F = 128
L = 2048
BIG = 1024
H = 64
A = 1024
D = 1536
TAPS = 31
EDGE = 16
TILE = 256
MESH = pl.DeviceIdType.MESH
f32, bf16, i32 = jnp.float32, jnp.bfloat16, jnp.int32


def rem(value, size):
    return lax.rem(value, size)


def loop(low, high, body):
    def step(i, carry):
        body(i)
        return carry

    lax.fori_loop(low, high, step, 0)


def times(value, size):
    return pl.multiple_of(value * size, size)


def dot(a, b, dims):
    return lax.dot_general(a, b, (dims, ((), ())), preferred_element_type=f32)


NT = ((1,), (1,))
NN = ((1,), (0,))
TN = ((0,), (0,))


class Exchange:
    def __init__(self, axis, me, send, recv, sems):
        self.axis, self.me, self.send, self.recv, self.sems = axis, me, send, recv, sems

    def copy(self, to, slot):
        return pltpu.make_async_remote_copy(
            src_ref=self.send(to),
            dst_ref=self.recv(slot),
            send_sem=self.sems.at[0, to],
            recv_sem=self.sems.at[1, slot],
            device_id={self.axis: to},
            device_id_type=MESH,
        )

    def start_to(self, to):
        self.copy(to, self.me).start()

    def start(self):
        loop(1, N, lambda k: self.start_to(rem(self.me + k, N)))

    def wait_recv(self):
        def one(k):
            source = rem(self.me + k, N)
            self.copy(source, source).wait_recv()

        loop(1, N, one)

    def wait_send(self):
        def one(k):
            to = rem(self.me + k, N)
            self.copy(to, self.me).wait_send()

        loop(1, N, one)


def kernel(
    q_ref, k_ref, v_ref, ids_ref, taps_ref, gain_ref, resid_hbm, cot_hbm, w_hbm,
    layer_ref, gresid_ref, dq_ref, dk_ref, dv_ref, wgrad_ref, ktaps_ref, ggain_ref,
    send1, recv1, ids_all, rot_qk, rot_v, qr, kr, vr, probs, out_rot, send2, recv2, attn,
    w_ref, resid_ref, cot_ref, stream, normed, pad, gpad, gshaped, gres, near_next, near_prev,
    edge_send, edge_recv, send3, recv3, rot_g, gr, dq_acc, dk_acc, dv_acc,
    two, own, core_send, core_recv, ring_send, ring_recv, total, part_send, part_recv,
    kpart, krecv, ksum, krecv2, kall,
    local_sem, sem1, sem_ids, sem2, sem3, sem4, edge_sem, core_sem, ring_sem, part_sem, ksem1, ksem2, ksem3,
):
    me, dp = lax.axis_index("seq"), lax.axis_index("dp")
    core, z = rem(dp, 2), dp // 2
    right, left = rem(me + 1, N), rem(me + N - 1, N)
    loads = [
        pltpu.make_async_copy(source, target, local_sem.at[i])
        for i, (source, target) in enumerate(
            ((w_hbm, w_ref), (resid_hbm, resid_ref), (cot_hbm, cot_ref))
        )
    ]
    for load in loads:
        load.start()

    barrier = pltpu.get_barrier_semaphore()

    def greet(k):
        pl.semaphore_signal(barrier, inc=1, device_id={"seq": rem(me + k, N)}, device_id_type=MESH)
        pl.semaphore_signal(barrier, inc=1, device_id={"dp": rem(dp + k, N)}, device_id_type=MESH)

    loop(1, N, greet)

    def pack_qkv(j):
        columns = pl.ds(times(j, 128), 128)
        qp, kp, vp = q_ref[:, columns], k_ref[:, columns], v_ref[:, columns]
        for half in range(2):
            c = slice(64 * half, 64 * half + 64)
            send1[2 * j + half, 0:F, :] = jnp.concatenate([qp[:, c], kp[:, c]], axis=1)
            send1[2 * j + half, F : F + 64, :] = jnp.concatenate([vp[0:64, c], vp[64:128, c]], axis=1)

    loop(0, N // 2, pack_qkv)
    ids_all[me] = jnp.broadcast_to(ids_ref[...], (8, F))
    pl.semaphore_wait(barrier, 2 * (N - 1))

    give_ids = Exchange("seq", me, lambda to: ids_all.at[me], lambda s: ids_all.at[s], sem_ids)
    give_qkv = Exchange("seq", me, lambda to: send1.at[to], lambda s: recv1.at[s], sem1)
    give_ids.start()
    give_qkv.start()
    recv1[me] = send1[me]
    give_ids.wait_recv()

    ids = ids_all[...]
    bounds = [jnp.int32(0)]
    for u in range(1, 6):
        bounds.append(jnp.sum(jnp.where(ids < u, 1, 0)) // 8)
    bounds.append(jnp.int32(L))
    start = jnp.int32(0)
    for u in range(6):
        start = start + jnp.where(bounds[u + 1] - bounds[u] == BIG, bounds[u], 0)
    marks = [(bounds[u] - start - BIG) & (L - 1) for u in range(6)]

    frame = me * F + lax.broadcasted_iota(i32, (F, 128), 0)
    low, high = jnp.zeros((F, 128), i32), jnp.full((F, 128), L, i32)
    for u in range(1, 6):
        low = jnp.maximum(low, jnp.where(bounds[u] <= frame, bounds[u], 0))
        high = jnp.minimum(high, jnp.where(bounds[u] > frame, bounds[u], L))
    near_next[...] = high - frame
    near_prev[...] = frame - low

    give_qkv.wait_recv()

    def widen(i):
        rot_qk[pl.ds(times(i, F), F), :] = recv1[i, 0:F, :].astype(f32)
        values = recv1[i, F : F + 64, :].astype(f32)
        rot_v[pl.ds(times(i, F), 64), :] = values[:, :64]
        rot_v[pl.ds(pl.multiple_of(i * F + 64, 64), 64), :] = values[:, 64:]

    loop(0, N, widen)
    rot_qk[L : L + F, :] = rot_qk[0:F, :]
    rot_v[L : L + F, :] = rot_v[0:F, :]

    def turn(i):
        at = (start + i * F) & (L - 1)
        rows = pl.ds(times(i, F), F)
        both = rot_qk[pl.ds(at, F), :]
        qr[rows, :] = (both[:, :64] * H**-0.5).astype(bf16)
        kr[rows, :] = both[:, 64:].astype(bf16)
        vr[rows, :] = rot_v[pl.ds(at, F), :].astype(bf16)

    loop(0, N, turn)

    column = lax.broadcasted_iota(i32, (1, BIG), 1)
    column_part = jnp.zeros((1, BIG), i32)
    for mark in marks:
        column_part = column_part + jnp.where(column >= mark, 1, 0)

    def attend(base, masked):
        def tile(t):
            rows = pl.ds(pl.multiple_of(base + t * TILE, TILE), TILE)
            scores = dot(qr[rows, :], kr[base : base + BIG, :], NT)
            if masked:
                row = t * TILE + lax.broadcasted_iota(i32, (TILE, 1), 0)
                row_part = jnp.zeros((TILE, 1), i32)
                for mark in marks:
                    row_part = row_part + jnp.where(row >= mark, 1, 0)
                scores = jnp.where(row_part == column_part, scores, -1e30)
            unnormed = jnp.exp(scores - jnp.max(scores, axis=1, keepdims=True))
            weights = (unnormed * (1.0 / jnp.sum(unnormed, axis=1, keepdims=True))).astype(bf16)
            probs[rows, :] = weights
            out_rot[rows, :] = dot(weights, vr[base : base + BIG, :], NN).astype(bf16).astype(f32)

        loop(0, BIG // TILE, tile)

    attend(0, False)
    attend(BIG, True)
    out_rot[L : L + F, :] = out_rot[0:F, :]

    give_out = Exchange("seq", me, lambda to: send2.at[to], lambda s: recv2.at[s], sem2)

    def pack_out(i):
        part = out_rot[pl.ds((i * F - start) & (L - 1), F), :]
        send2[i] = jnp.concatenate([part[0:64, :], part[64:128, :]], axis=1).astype(bf16)

    def send_out(k):
        to = rem(me + k, N)
        pack_out(to)
        give_out.start_to(to)

    loop(1, N, send_out)
    pack_out(me)
    recv2[me] = send2[me]
    give_out.wait_recv()

    def join(j):
        a, b = recv2[2 * j], recv2[2 * j + 1]
        columns = pl.ds(times(j, 128), 128)
        attn[0:64, columns] = jnp.concatenate([a[:, :64], b[:, :64]], axis=1)
        attn[64:128, columns] = jnp.concatenate([a[:, 64:], b[:, 64:]], axis=1)

    loop(0, N // 2, join)

    for load in loads:
        load.wait()

    def fold(value):
        return sum(value[:, 128 * c : 128 * c + 128] for c in range(value.shape[1] // 128))

    def project(c, squares):
        columns = pl.ds(times(c, 256), 256)
        part = resid_ref[:, columns].astype(f32) + dot(attn[...], w_ref[:, columns], NN)
        stream[:, columns] = part
        return squares + fold(part * part)

    squares = lax.fori_loop(0, D // 256, project, jnp.zeros((F, 128), f32))
    factor = lax.rsqrt(jnp.sum(squares, axis=1, keepdims=True) * (1.0 / D) + EPSILON)

    def norm(c):
        columns = pl.ds(times(c, 256), 256)
        part = stream[:, columns] * factor
        normed[:, columns] = part
        shaped = (part * gain_ref[:, columns]).astype(bf16)
        pad[EDGE : EDGE + F, columns] = shaped.astype(f32)
        edge_send[0, :, columns] = shaped[0:EDGE, :]
        edge_send[1, :, columns] = shaped[F - EDGE : F, :]

    loop(0, D // 256, norm)

    def edges(turn_of):
        def copy(side, to):
            return pltpu.make_async_remote_copy(
                src_ref=edge_send.at[2 * turn_of + side],
                dst_ref=edge_recv.at[2 * turn_of + side],
                send_sem=edge_sem.at[0, 2 * turn_of + side],
                recv_sem=edge_sem.at[1, 2 * turn_of + side],
                device_id={"seq": to},
                device_id_type=MESH,
            )

        return copy(0, left), copy(1, right)

    halo = edges(0)
    for copy in halo:
        copy.start()
    for copy in halo:
        copy.wait_recv()
    pad[EDGE + F :, :] = edge_recv[0].astype(f32)
    pad[0:EDGE, :] = edge_recv[1].astype(f32)

    def inside(step):
        if step > 0:
            return near_next[...] > step
        return near_prev[...] >= -step

    def convolve(c):
        columns = pl.ds(times(c, 128), 128)
        conv = jnp.zeros((F, 128), f32)
        for i in range(TAPS):
            step = i - TAPS // 2
            part = taps_ref[i : i + 1, columns] * pad[EDGE + step : EDGE + step + F, columns]
            conv = conv + (jnp.where(inside(step), part, 0.0) if step else part)
        sigma = 1.0 / (1.0 + jnp.exp(-conv))
        layer_ref[:, columns] = (stream[:, columns] + conv * sigma).astype(bf16)
        grad = cot_ref[:, columns].astype(f32) * sigma * (1.0 + conv * (1.0 - sigma))
        grad = grad.astype(bf16)
        gpad[EDGE : EDGE + F, columns] = grad.astype(f32)
        edge_send[2, :, columns] = grad[0:EDGE, :]
        edge_send[3, :, columns] = grad[F - EDGE : F, :]

    loop(0, D // 128, convolve)
    grad_halo = edges(1)
    for copy in grad_halo:
        copy.start()

    def kernel_rows(c):
        columns = pl.ds(times(c, 128), 128)
        grad = gpad[EDGE : EDGE + F, columns]
        for i in range(TAPS):
            step = i - TAPS // 2
            part = grad * pad[EDGE + step : EDGE + step + F, columns]
            if step:
                part = jnp.where(inside(step), part, 0.0)
            kpart[pl.ds(c * 32 + i, 1), :] = jnp.sum(part, axis=0, keepdims=True)

    loop(0, D // 128, kernel_rows)
    for copy in grad_halo:
        copy.wait_recv()
    gpad[EDGE + F :, :] = edge_recv[2].astype(f32)
    gpad[0:EDGE, :] = edge_recv[3].astype(f32)

    def convolve_back(c, dots):
        columns = pl.ds(times(c, 128), 128)
        grad = jnp.zeros((F, 128), f32)
        for i in range(TAPS):
            step = TAPS // 2 - i
            part = taps_ref[i : i + 1, columns] * gpad[EDGE + step : EDGE + step + F, columns]
            grad = grad + (jnp.where(inside(step), part, 0.0) if step else part)
        unit = normed[:, columns]
        kpart[pl.ds(c * 32 + TAPS, 1), :] = jnp.sum(grad * unit, axis=0, keepdims=True)
        scaled = grad * gain_ref[:, columns]
        gshaped[:, columns] = scaled
        return dots + scaled * unit

    dots = lax.fori_loop(0, D // 128, convolve_back, jnp.zeros((F, 128), f32))
    mean = jnp.sum(dots, axis=1, keepdims=True) * (1.0 / D)

    def kpiece(s):
        return pl.ds(pl.multiple_of(s * 24, 8), 24)

    ksum1 = Exchange("seq", me, lambda to: kpart.at[kpiece(to)], lambda s: krecv.at[s], ksem1)
    ksum1.start()

    def into_stream(c):
        columns = pl.ds(times(c, 256), 256)
        part = gshaped[:, columns] - normed[:, columns] * mean
        grad = (cot_ref[:, columns].astype(f32) + factor * part).astype(bf16)
        gres[:, columns] = grad
        gresid_ref[:, columns] = grad

    loop(0, D // 256, into_stream)

    give_grad = Exchange("seq", me, lambda to: send3.at[to], lambda s: recv3.at[s], sem3)

    def into_attn(j):
        grad = dot(gres[...], w_ref[pl.ds(times(j, 256), 256), :], NT).astype(bf16)
        for part in range(4):
            c = slice(64 * part, 64 * part + 64)
            send3[4 * j + part] = jnp.concatenate([grad[0:64, c], grad[64:128, c]], axis=1)

    loop(0, N // 4, into_attn)
    give_grad.start()
    recv3[me] = send3[me]

    def core_copy(j):
        return pltpu.make_async_remote_copy(
            src_ref=core_send.at[j],
            dst_ref=core_recv.at[j],
            send_sem=core_sem.at[0, j],
            recv_sem=core_sem.at[1, j],
            device_id={"dp": dp + 1 - 2 * core},
            device_id_type=MESH,
        )

    def project_grad(j):
        for c in range(D // 512):
            columns = slice(512 * c, 512 * c + 512)
            grad = dot(attn[:, pl.ds(times(j, 128), 128)], gres[:, columns], TN)
            two[0, :, columns] = grad[0:64, :]
            two[1, :, columns] = grad[64:128, :]
        own[j] = two[core]
        core_send[j] = two[1 - core].astype(bf16)
        core_copy(j).start()

    loop(0, N // 2, project_grad)

    ksum1.wait_recv()
    krecv[me] = kpart[kpiece(me), :]

    def add_up(ref):
        value = ref[0]
        for i in range(1, N):
            value = value + ref[i]
        return value

    ksum[...] = add_up(krecv)
    ksum2 = Exchange("dp", dp, lambda to: ksum, lambda s: krecv2.at[s], ksem2)
    ksum2.start()
    krecv2[dp] = ksum[...]

    give_grad.wait_recv()

    def widen_grad(i):
        values = recv3[i].astype(f32)
        rot_g[pl.ds(times(i, F), 64), :] = values[:, :64]
        rot_g[pl.ds(pl.multiple_of(i * F + 64, 64), 64), :] = values[:, 64:]

    loop(0, N, widen_grad)
    rot_g[L : L + F, :] = rot_g[0:F, :]

    def turn_grad(i):
        gr[pl.ds(times(i, F), F), :] = rot_g[pl.ds((start + i * F) & (L - 1), F), :].astype(bf16)

    loop(0, N, turn_grad)

    loop(0, N // 2, lambda j: core_copy(j).wait_recv())

    def ring_copy(way, s):
        return pltpu.make_async_remote_copy(
            src_ref=ring_send.at[way, s],
            dst_ref=ring_recv.at[way, s],
            send_sem=ring_sem.at[0, way, s],
            recv_sem=ring_sem.at[1, way, s],
            device_id={"dp": rem(dp + (2 if way == 0 else N - 2), N)},
            device_id_type=MESH,
        )

    half = D // 2

    def ring_step(s):
        for way in range(2):
            block = rem(z + 15 - s, 8) if way == 0 else rem(z + 1 + s, 8)
            columns = slice(half * way, half * way + half)
            value = own[block, :, columns] + core_recv[block, :, columns].astype(f32)
            ring_send[way, s] = value.astype(bf16)

            @pl.when(s > 0)
            def _():
                ring_copy(way, s - 1).wait_recv()
                ring_send[way, s] = (value + ring_recv[way, s - 1].astype(f32)).astype(bf16)

            ring_copy(way, s).start()

    dk_acc[...] = jnp.zeros((L, H), f32)
    dv_acc[...] = jnp.zeros((L, H), f32)

    def back(t):
        @pl.when(t < 7)
        def _():
            ring_step(t)

        rows = pl.ds(times(t, TILE), TILE)
        keys = pl.ds(times(t // (BIG // TILE), BIG), BIG)
        grad, weights = gr[rows, :], probs[rows, :]
        drift = dot(grad, vr[keys, :], NT)
        row_dot = jnp.sum(grad.astype(f32) * out_rot[rows, :], axis=1, keepdims=True)
        slope = (weights.astype(f32) * (drift - row_dot)).astype(bf16)
        dq_acc[rows, :] = dot(slope, kr[keys, :], NN) * H**-0.5
        dk_acc[keys, :] += dot(slope, qr[rows, :], TN)
        dv_acc[keys, :] += dot(weights, grad, TN)

    loop(0, L // TILE, back)

    give_qkv.wait_send()
    rot_qk[0:L, :] = jnp.concatenate([dq_acc[...], dk_acc[...]], axis=1)
    rot_v[0:L, :] = dv_acc[...]
    rot_qk[L : L + F, :] = rot_qk[0:F, :]
    rot_v[L : L + F, :] = rot_v[0:F, :]
    give_back = Exchange("seq", me, lambda to: send1.at[to], lambda s: recv4.at[s], sem4)
    recv4 = recv1

    def pack_back(i):
        at = (i * F - start) & (L - 1)
        send1[i, 0:F, :] = rot_qk[pl.ds(at, F), :].astype(bf16)
        part = rot_v[pl.ds(at, F), :]
        send1[i, F : F + 64, :] = jnp.concatenate([part[0:64, :], part[64:128, :]], axis=1).astype(bf16)

    def send_back(k):
        to = rem(me + k, N)
        pack_back(to)
        give_back.start_to(to)

    loop(1, N, send_back)
    pack_back(me)
    recv4[me] = send1[me]

    ksum2.wait_recv()
    kall[kpiece(me), :] = add_up(krecv2)
    ksum3 = Exchange("seq", me, lambda to: kall.at[kpiece(me)], lambda s: kall.at[kpiece(s)], ksem3)
    ksum3.start()

    value = own[z] + core_recv[z].astype(f32)
    for way in range(2):
        ring_copy(way, 6).wait_recv()
        columns = slice(half * way, half * way + half)
        total[:, columns] = value[:, columns] + ring_recv[way, 6].astype(f32)

    def pack_part(j):
        for c in range(D // 128):
            pair = total[pl.ds(times(j, 8), 8), 128 * c : 128 * c + 128]
            for k in range(2):
                two[k, 4 * c : 4 * c + 4, 0:128] = pair[4 * k : 4 * k + 4, :]
        for k in range(2):
            part_send[2 * j + k] = two[k, 0:48, 0:128].astype(bf16)

    loop(0, N // 2, pack_part)
    give_part = Exchange("seq", me, lambda to: part_send.at[to], lambda s: part_recv.at[s], part_sem)
    give_part.start()
    part_recv[me] = part_send[me]

    ksum3.wait_recv()
    for c in range(D // 128):
        columns = slice(128 * c, 128 * c + 128)
        ktaps_ref[:, columns] = kall[32 * c : 32 * c + TAPS, :]
        ggain_ref[:, columns] = kall[32 * c + TAPS : 32 * c + 32, :]

    give_back.wait_recv()

    def unpack(j):
        a, b = recv4[2 * j], recv4[2 * j + 1]
        columns = pl.ds(times(j, 128), 128)
        dq_ref[:, columns] = jnp.concatenate([a[0:F, :64], b[0:F, :64]], axis=1)
        dk_ref[:, columns] = jnp.concatenate([a[0:F, 64:], b[0:F, 64:]], axis=1)
        dv_ref[0:64, columns] = jnp.concatenate([a[F:, :64], b[F:, :64]], axis=1)
        dv_ref[64:128, columns] = jnp.concatenate([a[F:, 64:], b[F:, 64:]], axis=1)

    loop(0, N // 2, unpack)

    give_part.wait_recv()
    piece = part_recv[0].astype(f32)
    for i in range(1, N):
        piece = piece + part_recv[i].astype(f32)
    for c in range(D // 128):
        wgrad_ref[:, 128 * c : 128 * c + 128] = piece[4 * c : 4 * c + 4, :]

    for exchange in (give_ids, give_out, give_grad, give_back, ksum1, ksum2, ksum3, give_part):
        exchange.wait_send()
    for copy in halo + grad_halo:
        copy.wait_send()
    loop(0, N // 2, lambda j: core_copy(j).wait_send())

    def ring_done(s):
        for way in range(2):
            ring_copy(way, s).wait_send()

    loop(0, 7, ring_done)


def local(resid, query, key, value, out_weight, conv_kernel, conv_gain, recording_ids, cotangent):
    vmem = pl.BlockSpec(memory_space=pltpu.VMEM)
    hbm = pl.BlockSpec(memory_space=pl.ANY)
    scratch = [
        pltpu.VMEM((N, 192, 128), bf16),
        pltpu.VMEM((N, 192, 128), bf16),
        pltpu.VMEM((N, 8, 128), i32),
        pltpu.VMEM((L + F, 128), f32),
        pltpu.VMEM((L + F, H), f32),
        pltpu.VMEM((L, H), bf16),
        pltpu.VMEM((L, H), bf16),
        pltpu.VMEM((L, H), bf16),
        pltpu.VMEM((L, BIG), bf16),
        pltpu.VMEM((L + F, H), f32),
        pltpu.VMEM((N, 64, 128), bf16),
        pltpu.VMEM((N, 64, 128), bf16),
        pltpu.VMEM((F, A), bf16),
        pltpu.VMEM((A, D), bf16),
        pltpu.VMEM((F, D), bf16),
        pltpu.VMEM((F, D), bf16),
        pltpu.VMEM((F, D), f32),
        pltpu.VMEM((F, D), f32),
        pltpu.VMEM((F + 2 * EDGE, D), f32),
        pltpu.VMEM((F + 2 * EDGE, D), f32),
        pltpu.VMEM((F, D), f32),
        pltpu.VMEM((F, D), bf16),
        pltpu.VMEM((F, 128), i32),
        pltpu.VMEM((F, 128), i32),
        pltpu.VMEM((4, EDGE, D), bf16),
        pltpu.VMEM((4, EDGE, D), bf16),
        pltpu.VMEM((N, 64, 128), bf16),
        pltpu.VMEM((N, 64, 128), bf16),
        pltpu.VMEM((L + F, H), f32),
        pltpu.VMEM((L, H), bf16),
        pltpu.VMEM((L, H), f32),
        pltpu.VMEM((L, H), f32),
        pltpu.VMEM((L, H), f32),
        pltpu.VMEM((2, 64, D), f32),
        pltpu.VMEM((8, 64, D), f32),
        pltpu.VMEM((8, 64, D), bf16),
        pltpu.VMEM((8, 64, D), bf16),
        pltpu.VMEM((2, 7, 64, D // 2), bf16),
        pltpu.VMEM((2, 7, 64, D // 2), bf16),
        pltpu.VMEM((64, D), f32),
        pltpu.VMEM((N, 48, 128), bf16),
        pltpu.VMEM((N, 48, 128), bf16),
        pltpu.VMEM((384, 128), f32),
        pltpu.VMEM((N, 24, 128), f32),
        pltpu.VMEM((24, 128), f32),
        pltpu.VMEM((N, 24, 128), f32),
        pltpu.VMEM((384, 128), f32),
        pltpu.SemaphoreType.DMA((3,)),
        pltpu.SemaphoreType.DMA((2, N)),
        pltpu.SemaphoreType.DMA((2, N)),
        pltpu.SemaphoreType.DMA((2, N)),
        pltpu.SemaphoreType.DMA((2, N)),
        pltpu.SemaphoreType.DMA((2, N)),
        pltpu.SemaphoreType.DMA((2, 4)),
        pltpu.SemaphoreType.DMA((2, 8)),
        pltpu.SemaphoreType.DMA((2, 2, 7)),
        pltpu.SemaphoreType.DMA((2, N)),
        pltpu.SemaphoreType.DMA((2, N)),
        pltpu.SemaphoreType.DMA((2, N)),
        pltpu.SemaphoreType.DMA((2, N)),
    ]
    outs = pl.pallas_call(
        kernel,
        out_shape=(
            jax.ShapeDtypeStruct((F, D), bf16),
            jax.ShapeDtypeStruct((F, D), bf16),
            jax.ShapeDtypeStruct((F, A), bf16),
            jax.ShapeDtypeStruct((F, A), bf16),
            jax.ShapeDtypeStruct((F, A), bf16),
            jax.ShapeDtypeStruct((4, D), f32),
            jax.ShapeDtypeStruct((TAPS, D), f32),
            jax.ShapeDtypeStruct((1, D), f32),
        ),
        in_specs=[vmem] * 6 + [hbm] * 3,
        out_specs=(vmem,) * 8,
        scratch_shapes=scratch,
        compiler_params=pltpu.CompilerParams(
            collective_id=0, has_side_effects=True, vmem_limit_bytes=56 * 1024 * 1024
        ),
        name="conformer",
    )(
        query[0], key[0], value[0], recording_ids, conv_kernel, conv_gain[None],
        resid[0], cotangent[0], out_weight,
    )
    layer_out, grad_resid, grad_q, grad_k, grad_v, grad_w, grad_taps, grad_gain = outs
    return (
        layer_out[None], grad_resid[None], grad_q[None], grad_k[None], grad_v[None],
        grad_w, grad_taps, grad_gain[0],
    )


def solution(mesh):
    rows = P("dp", "seq", None)
    return jax.shard_map(
        local,
        mesh=mesh,
        in_specs=(rows, rows, rows, rows, P(), P(), P(), P("dp", "seq"), rows),
        out_specs=(rows, rows, rows, rows, rows, P(("dp", "seq"), None), P(), P()),
        check_vma=False,
    )
```

time: 605 us -> 130 us (0.21); the launches traced: 596 us -> 129 us
  waiting for transfers between devices: 224 us -> 0 us
  blocking collectives: 162 us -> 0 us
  Pallas kernels: 0 us -> 116 us
  matrix products: 66.7 us -> 0 us
  local copies, waits for them, and re-layouts: 72.7 us -> 11.1 us
  other arithmetic: 40.8 us -> 1.35 us
  starting transfers between devices: 15.3 us -> 0 us
  between operations: 15.1 us -> 0.66 us
    all_gather x4 -> x0, waiting for transfers between devices: 127 us -> none  [the longest x1 56.7 us: local(): grad_piece = lax.all_gather(grad_attn, 'seq', axis=0, tiled=True)]
    pallas_call x0 -> x1, Pallas kernels: none -> 116 us  [local(): pl.pallas_call(kernel, out_shape=(jax.ShapeDtypeStruct((F, D), bf16), jax...]
    unnamed x6 -> x0, waiting for transfers between devices: 92.8 us -> none
    all_gather x4 -> x0, blocking collectives: 88.1 us -> none  [the longest x1 24 us: local(): lax.all_gather(row_dot, 'seq', axis=1, tiled=True)]
    psum x1 -> x0, blocking collectives: 74.1 us -> none  [local(): kernel_sum, gain_sum = lax.psum((kernel_part, gain_part), ('dp', 'seq'))]
    dot_general x9 -> x0, matrix products: 66.7 us -> none  [the longest x1 14 us: backward_block(): jnp.einsum('hae,hbe->hab', q_part, k_heads, preferred_element_type=jnp.fl...]
    reduce_sum x9 -> x0, other arithmetic: 34.8 us -> none  [the longest x6 21.5 us: local(): jnp.sum(jnp.where(match_fore, grad_conv.astype(jnp.float32) * shaped_pad[...]
    all_gather x4 -> x0, local copies, waits for them, and re-layouts: 26.1 us -> none  [the longest x1 6.58 us: local(): q_piece = lax.all_gather(q_rows, 'seq', axis=0, tiled=True)]
  transfers between devices with their start and end apart: 9 -> 0, of which waited for: 5 -> 0; matrix products, arithmetic and copies ran while one was open for 24% -> 0% of each run, Pallas kernels for 0% -> 0%
where the time goes in v1:
time: 130 us; the launch traced here: 129 us
  Pallas kernels  116 us (89%)
  local copies, waits for them, and re-layouts  11.1 us (9%)
  other arithmetic  1.35 us (1%)
    pallas_call x1, Pallas kernels, local(): pl.pallas_call(kernel, out_shape=(jax.ShapeDtypeStruct((F, D), bf16), jax...  116 us
    unnamed x11, local copies, waits for them, and re-layouts  9.83 us

profile of v1, /device:TPU:8, one launch (start us, length us, event | category | flops | bytes accessed | tf_op | source)
XLA Modules:
  0.0 129.3 jit_solution(1817493632903090723)
XLA Ops:
  0.6 1.3 %broadcast_in_dim.18.gain_ref = f32[1,1536]{1,0:T(1,128)} reshape(f32[1536]{0:T(1024)} %param.15) | data formatting | bytes 12288 | tf_op jit(solution)/shard_map/broadcast_in_dim | solution.py:622
  1.9 116.2 %conformer.1 = (bf16[128,1536]{1,0:T(8,128)(2,1)}, bf16[128,1536]{1,0:T(8,128)(2,1)}, bf16[128,1024]{1,0:T(8,128)(2,1)}, bf16[128,1024]{1,0:T(8,128)(2,1)}, bf16...) custom-call(bf16[128,1024]{1,0:T(8,128)(2,1)} %bitcast.14, ...), custom_call_target="tpu_custom_call" | custom-call | tf_op jit(solution)/shard_map/conformer/pallas_call | solution.py:602
  118.1 0.0 copy-start.1
  118.2 0.0 copy-start
  118.2 1.4 %reduce = f32[1536]{0:T(1024)} reduce(f32[1,1536]{1,0:T(1,128)} %get-tuple-element.23, f32[]{:T(128)} %constant.6), dimensions={0}, to_apply=%get-tuple-element.23.reduce_sub_computation | reduce | bytes 12292 | tf_op jit(solution)/shard_map/conformer/pallas_call | solution.py:602
  119.5 1.8 %copy.24 = bf16[1,128,1536]{2,1,0:T(8,128)(2,1)} copy(bf16[1,128,1536]{2,1,0:T(8,128)(2,1)} %bitcast.11) | data formatting | bytes 786432
  121.3 1.8 %copy.25 = bf16[1,128,1536]{2,1,0:T(8,128)(2,1)} copy(bf16[1,128,1536]{2,1,0:T(8,128)(2,1)} %bitcast.10) | data formatting | bytes 786432
  123.0 1.7 %copy.26 = bf16[1,128,1024]{2,1,0:T(8,128)(2,1)} copy(bf16[1,128,1024]{2,1,0:T(8,128)(2,1)} %bitcast.19) | data formatting | bytes 524288
  124.7 1.7 %copy.27 = bf16[1,128,1024]{2,1,0:T(8,128)(2,1)} copy(bf16[1,128,1024]{2,1,0:T(8,128)(2,1)} %bitcast.18) | data formatting | bytes 524288
  126.4 1.7 %copy.28 = bf16[1,128,1024]{2,1,0:T(8,128)(2,1)} copy(bf16[1,128,1024]{2,1,0:T(8,128)(2,1)} %bitcast.17) | data formatting | bytes 524288
  128.1 0.0 copy-done.1
  128.1 0.6 copy.29
  128.7 0.0 copy-done
  128.7 0.7 copy.30
Async XLA Ops:
  118.1 9.9 %copy-start.1 = (f32[4,1536]{1,0:T(4,128)S(1)}, f32[4,1536]{1,0:T(4,128)}, u32[]{:S(2)}) copy-start(f32[4,1536]{1,0:T(4,128)} %get-tuple-element.37) | copy-start | bytes 73732
  118.2 10.5 %copy-start = (f32[31,1536]{1,0:T(8,128)S(1)}, f32[31,1536]{1,0:T(8,128)}, u32[]{:S(2)}) copy-start(f32[31,1536]{1,0:T(8,128)} %get-tuple-element.38) | copy-start | bytes 571396

commit v2 on v1

v2 whole, which is shorter than its diff:
```python
import jax
import jax.numpy as jnp
from jax import lax
from jax.experimental import pallas as pl
from jax.experimental.pallas import tpu as pltpu
from jax.sharding import PartitionSpec as P

EPSILON = 1e-05
N = 16
F = 128
L = 2048
BIG = 1024
H = 64
A = 1024
D = 1536
TAPS = 31
EDGE = 16
TILE = 256
SPLIT = 1024
MESH = pl.DeviceIdType.MESH
f32, bf16, i32 = jnp.float32, jnp.bfloat16, jnp.int32


def rem(value, size):
    return lax.rem(value, size)


def loop(low, high, body):
    def step(i, carry):
        body(i)
        return carry

    lax.fori_loop(low, high, step, 0)


def times(value, size):
    return pl.multiple_of(value * size, size)


def dot(a, b, dims):
    return lax.dot_general(a, b, (dims, ((), ())), preferred_element_type=f32)


NT = ((1,), (1,))
NN = ((1,), (0,))
TN = ((0,), (0,))


class Copies:
    def __init__(self, flights, count, copy):
        self.count, self.copy, self.received = count, copy, False
        flights.append(self)

    def start(self, i):
        self.copy(i).start()

    def wait_recv(self):
        self.received = True
        loop(0, self.count, lambda i: self.copy(i).wait_recv())

    def wait_send(self):
        loop(0, self.count, lambda i: self.copy(i).wait_send())


class Exchange:
    def __init__(self, flights, device, count, me, send, recv, sems):
        self.device, self.count, self.me = device, count, me
        self.send, self.recv, self.sems = send, recv, sems
        self.received = False
        flights.append(self)

    def copy(self, to, slot):
        return pltpu.make_async_remote_copy(
            src_ref=self.send(to),
            dst_ref=self.recv(slot),
            send_sem=self.sems.at[0, to],
            recv_sem=self.sems.at[1, slot],
            device_id=self.device(to),
            device_id_type=MESH,
        )

    def others(self, body):
        loop(1, self.count, lambda k: body(rem(self.me + k, self.count)))

    def start_to(self, to):
        self.copy(to, self.me).start()

    def start(self):
        self.others(self.start_to)

    def wait_recv(self):
        self.received = True
        self.others(lambda source: self.copy(source, source).wait_recv())

    def wait_send(self):
        self.others(lambda to: self.copy(to, self.me).wait_send())


def kernel(
    q_hbm, k_hbm, v_hbm, ids_ref, taps_hbm, gain_in, resid_hbm, cot_hbm, w_hbm,
    layer_hbm, gresid_hbm, dq_hbm, dk_hbm, dv_hbm, wgrad_ref, ktaps_ref, ggain_ref,
    q_ref, k_ref, v_ref, taps_ref, gain_ref, layer_ref, dq_ref, dk_ref, dv_ref, shift, gshift, send0, recv0,
    send1, recv1, ids_all, rot_qk, rot_v, qr, kr, vr, probs, out_rot, send2, recv2, attn,
    w_ref, resid_ref, cot_ref, stream, normed, pad, gpad, gshaped, gres, near_next, near_prev, dots_ref,
    edge_send, edge_recv, send3, recv3, send4, recv4, rot_g, gr, kv_acc,
    two, own, core_send, core_recv, z_send, z_recv, seq_send, seq_recv, z_send2, z_recv2, seq_send2, seq_recv2,
    kpart, krecv, ksum, krecv2, kall,
    local_sem, sem0, sem1, sem_ids, sem2, sem3, sem4, edge_sem, core_sem, z_sem, seq_sem, z_sem2, seq_sem2, ksem1, ksem2, ksem3,
):
    flights = []
    me, dp = lax.axis_index("seq"), lax.axis_index("dp")
    core, z = rem(dp, 2), dp // 2
    over_seq = (lambda to: {"seq": to}), N, me
    over_dp = (lambda to: {"dp": to}), N, dp
    over_z = (lambda to: {"dp": 2 * to + core}), N // 2, z
    pairs = (
        (q_hbm, q_ref), (k_hbm, k_ref), (v_hbm, v_ref),
        (w_hbm, w_ref), (resid_hbm, resid_ref), (cot_hbm, cot_ref), (taps_hbm, taps_ref),
        (layer_ref, layer_hbm), (gres, gresid_hbm), (dq_ref, dq_hbm), (dk_ref, dk_hbm), (dv_ref, dv_hbm),
    )
    moves = [pltpu.make_async_copy(a, b, local_sem.at[i]) for i, (a, b) in enumerate(pairs)]
    first, loads, stores = moves[:3], moves[3:7], moves[7:]
    for load in first + loads:
        load.start()
    gain_ref[0, :] = gain_in[...]

    barrier = pltpu.get_barrier_semaphore()

    def greet(k):
        pl.semaphore_signal(barrier, inc=1, device_id={"seq": rem(me + k, N)}, device_id_type=MESH)
        pl.semaphore_signal(barrier, inc=1, device_id={"dp": rem(dp + k, N)}, device_id_type=MESH)

    loop(1, N, greet)

    for load in first:
        load.wait()

    def pack_qkv(j):
        columns = pl.ds(times(j, 128), 128)
        qp, kp, vp = q_ref[:, columns], k_ref[:, columns], v_ref[:, columns]
        for half in range(2):
            c = slice(64 * half, 64 * half + 64)
            send0[2 * j + half] = jnp.concatenate([qp[:, c], kp[:, c]], axis=1)
            send1[2 * j + half] = jnp.concatenate([vp[0:64, c], vp[64:128, c]], axis=1)

    loop(0, N // 2, pack_qkv)
    ids_all[me] = jnp.broadcast_to(ids_ref[...], (8, F))
    pl.semaphore_wait(barrier, 2 * (N - 1))

    give_ids = Exchange(flights, *over_seq, lambda to: ids_all.at[me], lambda s: ids_all.at[s], sem_ids)
    give_qk = Exchange(flights, *over_seq, lambda to: send0.at[to], lambda s: recv0.at[s], sem0)
    give_v = Exchange(flights, *over_seq, lambda to: send1.at[to], lambda s: recv1.at[s], sem1)
    give_ids.start()
    give_qk.start()
    give_v.start()
    recv0[me] = send0[me]
    recv1[me] = send1[me]
    give_ids.wait_recv()

    ids = ids_all[...]
    bounds = [jnp.int32(0)]
    for u in range(1, 6):
        bounds.append(jnp.sum(jnp.where(ids < u, 1, 0)) // 8)
    bounds.append(jnp.int32(L))
    start = jnp.int32(0)
    for u in range(6):
        start = start + jnp.where(bounds[u + 1] - bounds[u] == BIG, bounds[u], 0)
    marks = [(bounds[u] - start - BIG) & (L - 1) for u in range(6)]

    frame = me * F + lax.broadcasted_iota(i32, (F, 128), 0)
    low, high = jnp.zeros((F, 128), i32), jnp.full((F, 128), L, i32)
    for u in range(1, 6):
        low = jnp.maximum(low, jnp.where(bounds[u] <= frame, bounds[u], 0))
        high = jnp.minimum(high, jnp.where(bounds[u] > frame, bounds[u], L))
    near_next[...] = high - frame
    near_prev[...] = frame - low

    give_qk.wait_recv()

    def widen(i):
        rot_qk[pl.ds(times(i, F), F), :] = recv0[i].astype(f32)

    loop(0, N, widen)
    rot_qk[L : L + F, :] = rot_qk[0:F, :]

    def turn(i):
        rows = pl.ds(times(i, F), F)
        both = rot_qk[pl.ds((start + i * F) & (L - 1), F), :]
        qr[rows, :] = (both[:, :64] * H**-0.5).astype(bf16)
        kr[rows, :] = both[:, 64:].astype(bf16)

    loop(0, N, turn)

    column = lax.broadcasted_iota(i32, (1, BIG), 1)
    column_part = jnp.zeros((1, BIG), i32)
    for mark in marks:
        column_part = column_part + jnp.where(column >= mark, 1, 0)

    def weigh(base, masked):
        def tile(t):
            rows = pl.ds(pl.multiple_of(base + t * TILE, TILE), TILE)
            scores = dot(qr[rows, :], kr[base : base + BIG, :], NT)
            if masked:
                row = t * TILE + lax.broadcasted_iota(i32, (TILE, 1), 0)
                row_part = jnp.zeros((TILE, 1), i32)
                for mark in marks:
                    row_part = row_part + jnp.where(row >= mark, 1, 0)
                scores = jnp.where(row_part == column_part, scores, -1e30)
            unnormed = jnp.exp(scores - jnp.max(scores, axis=1, keepdims=True))
            probs[rows, :] = (unnormed * (1.0 / jnp.sum(unnormed, axis=1, keepdims=True))).astype(bf16)

        loop(0, BIG // TILE, tile)

    weigh(0, False)
    weigh(BIG, True)

    give_v.wait_recv()

    def widen_v(i):
        values = recv1[i].astype(f32)
        rot_v[pl.ds(times(i, F), 64), :] = values[:, :64]
        rot_v[pl.ds(pl.multiple_of(i * F + 64, 64), 64), :] = values[:, 64:]

    loop(0, N, widen_v)
    rot_v[L : L + F, :] = rot_v[0:F, :]

    def turn_v(i):
        vr[pl.ds(times(i, F), F), :] = rot_v[pl.ds((start + i * F) & (L - 1), F), :].astype(bf16)

    loop(0, N, turn_v)

    def mix(t):
        rows = pl.ds(times(t, TILE), TILE)
        keys = pl.ds(times(t // (BIG // TILE), BIG), BIG)
        out_rot[rows, :] = dot(probs[rows, :], vr[keys, :], NN).astype(bf16).astype(f32)

    loop(0, L // TILE, mix)
    out_rot[L : L + F, :] = out_rot[0:F, :]

    give_out = Exchange(flights, *over_seq, lambda to: send2.at[to], lambda s: recv2.at[s], sem2)

    def pack_out(i):
        part = out_rot[pl.ds((i * F - start) & (L - 1), F), :]
        send2[i] = jnp.concatenate([part[0:64, :], part[64:128, :]], axis=1).astype(bf16)

    def send_out(k):
        to = rem(me + k, N)
        pack_out(to)
        give_out.start_to(to)

    loop(1, N, send_out)
    pack_out(me)
    recv2[me] = send2[me]
    give_out.wait_recv()

    def join(j):
        a, b = recv2[2 * j], recv2[2 * j + 1]
        columns = pl.ds(times(j, 128), 128)
        for k, (first, second) in enumerate(((a, b), (b, a))):
            attn[k, 0:64, columns] = jnp.concatenate([first[:, :64], second[:, :64]], axis=1)
            attn[k, 64:128, columns] = jnp.concatenate([first[:, 64:], second[:, 64:]], axis=1)

    loop(0, N // 2, join)

    for load in loads:
        load.wait()

    def fold(value):
        return sum(value[:, 128 * c : 128 * c + 128] for c in range(value.shape[1] // 128))

    def project(c, squares):
        columns = pl.ds(times(c, 256), 256)
        part = resid_ref[:, columns].astype(f32) + dot(attn[0], w_ref[:, columns], NN)
        stream[:, columns] = part
        return squares + fold(part * part)

    squares = lax.fori_loop(0, D // 256, project, jnp.zeros((F, 128), f32))
    factor = lax.rsqrt(jnp.sum(squares, axis=1, keepdims=True) * (1.0 / D) + EPSILON)

    def norm(c):
        columns = pl.ds(times(c, 256), 256)
        part = stream[:, columns] * factor
        normed[:, columns] = part
        shaped = (part * gain_ref[:, columns]).astype(bf16)
        pad[EDGE : EDGE + F, columns] = shaped.astype(f32)
        edge_send[0, :, columns] = shaped[0:EDGE, :]
        edge_send[1, :, columns] = shaped[F - EDGE : F, :]

    loop(0, D // 256, norm)

    def edges(turn_of):
        def copy(side):
            return pltpu.make_async_remote_copy(
                src_ref=edge_send.at[2 * turn_of + side],
                dst_ref=edge_recv.at[2 * turn_of + side],
                send_sem=edge_sem.at[0, 2 * turn_of + side],
                recv_sem=edge_sem.at[1, 2 * turn_of + side],
                device_id={"seq": rem(me + jnp.where(side == 0, N - 1, 1), N)},
                device_id_type=MESH,
            )

        return Copies(flights, 2, copy)

    halo = edges(0)
    halo.start(0)
    halo.start(1)

    def shift_rows(source, target, low, high):
        def one(c):
            columns = pl.ds(times(c, 128), 128)
            for s in range(8):
                target[s, low:high, columns] = source[low + s + 1 : high + s + 1, columns]

        loop(0, D // 128, one)

    shift_rows(pad, shift, 16, 128)

    def inside(step, rows):
        if step > 0:
            return near_next[rows, :] > step
        return near_prev[rows, :] >= -step

    def over_taps(source, low, count, wide, first_column, mirrored):
        rows = slice(low, low + count)
        sums = [jnp.zeros((count, 128), f32)] * wide
        for i in range(TAPS):
            step = i - TAPS // 2
            mask = inside(step, rows)
            at = slice(low + i // 8 * 8, low + i // 8 * 8 + count)
            tap = TAPS - 1 - i if mirrored else i
            for k in range(wide):
                columns = pl.ds(pl.multiple_of(first_column + 128 * k, 128), 128)
                part = taps_ref[tap : tap + 1, columns] * source[i % 8, at, columns]
                sums[k] = sums[k] + (jnp.where(mask, part, 0.0) if step else part)
        return sums

    WIDE, TALL = 2, 64

    def convolve(low, tall):
        rows = slice(low, low + tall)

        def one(c):
            sums = over_taps(shift, low, tall, WIDE, c * 128 * WIDE, False)
            for k in range(WIDE):
                columns = pl.ds(pl.multiple_of(c * 128 * WIDE + 128 * k, 128), 128)
                conv = sums[k]
                sigma = 1.0 / (1.0 + jnp.exp(-conv))
                layer_ref[rows, columns] = (stream[rows, columns] + conv * sigma).astype(bf16)
                grad = cot_ref[rows, columns].astype(f32) * sigma * (1.0 + conv * (1.0 - sigma))
                grad = grad.astype(bf16)
                gpad[EDGE + low : EDGE + low + tall, columns] = grad.astype(f32)
                if low == 0:
                    edge_send[2, :, columns] = grad[0:EDGE, :]
                if low + tall == F:
                    edge_send[3, :, columns] = grad[tall - EDGE : tall, :]

        loop(0, D // (128 * WIDE), one)

    convolve(32, 64)
    halo.wait_recv()
    pad[EDGE + F :, :] = edge_recv[0].astype(f32)
    pad[0:EDGE, :] = edge_recv[1].astype(f32)
    shift_rows(pad, shift, 0, 16)
    shift_rows(pad, shift, 128, 152)

    convolve(0, 32)
    convolve(96, 32)
    grad_halo = edges(1)
    grad_halo.start(0)
    grad_halo.start(1)
    stores[0].start()

    shift_rows(gpad, gshift, 16, 128)

    def kernel_rows(c):
        for i in range(TAPS):
            step = i - TAPS // 2
            mask = inside(step, slice(0, F))
            for k in range(WIDE):
                columns = pl.ds(pl.multiple_of(c * 128 * WIDE + 128 * k, 128), 128)
                part = gpad[EDGE : EDGE + F, columns] * shift[i % 8, i // 8 * 8 : i // 8 * 8 + F, columns]
                if step:
                    part = jnp.where(mask, part, 0.0)
                kpart[pl.ds((c * WIDE + k) * 32 + i, 1), :] = jnp.sum(part, axis=0, keepdims=True)

    loop(0, D // (128 * WIDE), kernel_rows)
    grad_halo.wait_recv()
    gpad[EDGE + F :, :] = edge_recv[2].astype(f32)
    gpad[0:EDGE, :] = edge_recv[3].astype(f32)
    shift_rows(gpad, gshift, 0, 16)
    shift_rows(gpad, gshift, 128, 152)

    dots_ref[...] = jnp.zeros((F, 128), f32)

    def convolve_back(c):
        gains = [jnp.zeros((1, 128), f32)] * WIDE
        for low in range(0, F, TALL):
            rows = slice(low, low + TALL)
            sums = over_taps(gshift, low, TALL, WIDE, c * 128 * WIDE, True)
            for k in range(WIDE):
                columns = pl.ds(pl.multiple_of(c * 128 * WIDE + 128 * k, 128), 128)
                unit = normed[rows, columns]
                gains[k] = gains[k] + jnp.sum(sums[k] * unit, axis=0, keepdims=True)
                scaled = sums[k] * gain_ref[:, columns]
                gshaped[rows, columns] = scaled
                dots_ref[rows, :] += scaled * unit
        for k in range(WIDE):
            kpart[pl.ds((c * WIDE + k) * 32 + TAPS, 1), :] = gains[k]

    loop(0, D // (128 * WIDE), convolve_back)
    mean = jnp.sum(dots_ref[...], axis=1, keepdims=True) * (1.0 / D)

    def kpiece(s):
        return pl.ds(pl.multiple_of(s * 24, 8), 24)

    ksum1 = Exchange(flights, *over_seq, lambda to: kpart.at[kpiece(to)], lambda s: krecv.at[s], ksem1)
    ksum1.start()

    def into_stream(c):
        columns = pl.ds(times(c, 256), 256)
        part = gshaped[:, columns] - normed[:, columns] * mean
        grad = (cot_ref[:, columns].astype(f32) + factor * part).astype(bf16)
        gres[:, columns] = grad

    loop(0, D // 256, into_stream)
    stores[1].start()

    give_grad = Exchange(flights, *over_seq, lambda to: send3.at[to], lambda s: recv3.at[s], sem3)

    def into_attn(j):
        grad = dot(gres[...], w_ref[pl.ds(times(j, 256), 256), :], NT).astype(bf16)
        for part in range(4):
            c = slice(64 * part, 64 * part + 64)
            send3[4 * j + part] = jnp.concatenate([grad[0:64, c], grad[64:128, c]], axis=1)

    loop(0, N // 4, into_attn)
    give_grad.start()
    recv3[me] = send3[me]

    def core_copy(j):
        return pltpu.make_async_remote_copy(
            src_ref=core_send.at[j],
            dst_ref=core_recv.at[j],
            send_sem=core_sem.at[0, j],
            recv_sem=core_sem.at[1, j],
            device_id={"dp": dp + 1 - 2 * core},
            device_id_type=MESH,
        )

    to_core = Copies(flights, N // 2, core_copy)

    def project_grad(j):
        pair = attn[core, :, pl.ds(times(j, 128), 128)]
        for c in range(D // 512):
            columns = slice(512 * c, 512 * c + 512)
            grad = dot(pair, gres[:, columns], TN)
            own[j, :, columns] = grad[0:64, :]
            core_send[j, :, columns] = grad[64:128, :].astype(bf16)
        to_core.start(j)

    loop(0, N // 2, project_grad)

    give_grad.wait_recv()

    def widen_grad(i):
        values = recv3[i].astype(f32)
        rot_g[pl.ds(times(i, F), 64), :] = values[:, :64]
        rot_g[pl.ds(pl.multiple_of(i * F + 64, 64), 64), :] = values[:, 64:]

    loop(0, N, widen_grad)
    rot_g[L : L + F, :] = rot_g[0:F, :]

    def turn_grad(i):
        gr[pl.ds(times(i, F), F), :] = rot_g[pl.ds((start + i * F) & (L - 1), F), :].astype(bf16)

    loop(0, N, turn_grad)

    ksum1.wait_recv()
    krecv[me] = kpart[kpiece(me), :]

    def add_up(ref):
        value = ref[0].astype(f32)
        for i in range(1, ref.shape[0]):
            value = value + ref[i].astype(f32)
        return value

    ksum[...] = add_up(krecv)
    ksum2 = Exchange(flights, *over_dp, lambda to: ksum, lambda s: krecv2.at[s], ksem2)
    ksum2.start()
    krecv2[dp] = ksum[...]
    to_core.wait_recv()

    z_first = Exchange(flights, *over_z, lambda to: z_send.at[to], lambda s: z_recv.at[s], z_sem)

    def add_core(k):
        to = rem(z + k, N // 2)
        value = own[to] + core_recv[to].astype(f32)
        own[to, :, 0:SPLIT] = value[:, 0:SPLIT]
        z_send[to] = value[:, SPLIT:].astype(bf16)

        @pl.when(k < N // 2)
        def _():
            z_first.start_to(to)

    loop(1, N // 2 + 1, add_core)
    z_recv[z] = z_send[z]

    def pack_seq(j):
        for b in range(N // 2):
            pair = own[b, pl.ds(times(j, 8), 8), 0:SPLIT]
            for k in range(2):
                two[k, 4 * b : 4 * b + 4, :] = pair[4 * k : 4 * k + 4, :]
        for k in range(2):
            seq_send[2 * j + k] = two[k].astype(bf16)

    loop(0, N // 2, pack_seq)
    seq_first = Exchange(flights, *over_seq, lambda to: seq_send.at[to], lambda s: seq_recv.at[s], seq_sem)
    seq_first.start()
    seq_recv[me] = seq_send[me]

    kv_acc[...] = jnp.zeros((2 * H, L), f32)

    def back(t):
        rows = pl.ds(times(t, TILE), TILE)
        keys = pl.ds(times(t // (BIG // TILE), BIG), BIG)
        grad, weights = gr[rows, :], probs[rows, :]
        drift = dot(grad, vr[keys, :], NT)
        row_dot = jnp.sum(grad.astype(f32) * out_rot[rows, :], axis=1, keepdims=True)
        slope = (weights.astype(f32) * (drift - row_dot)).astype(bf16)
        rot_v[rows, :] = dot(slope, kr[keys, :], NN) * H**-0.5
        kv_acc[0:H, keys] += dot(qr[rows, :], slope, TN)
        kv_acc[H:, keys] += dot(grad, weights, TN)

    loop(0, L // TILE, back)

    ksum2.wait_recv()
    kall[kpiece(me), :] = add_up(krecv2)
    ksum3 = Exchange(flights, *over_seq, lambda to: kall.at[kpiece(me)], lambda s: kall.at[kpiece(s)], ksem3)
    ksum3.start()

    def upright(i):
        rows = pl.ds(times(i, F), F)
        rot_qk[rows, :] = kv_acc[:, rows].T

    loop(0, N, upright)
    rot_qk[L : L + F, :] = rot_qk[0:F, :]
    rot_v[L : L + F, :] = rot_v[0:F, :]
    give_back = Exchange(flights, *over_seq, lambda to: send4.at[to], lambda s: recv4.at[s], sem4)

    def pack_back(i):
        at = (i * F - start) & (L - 1)
        send4[i, 0:F, :] = rot_qk[pl.ds(at, F), :].astype(bf16)
        part = rot_v[pl.ds(at, F), :]
        send4[i, F : F + 64, :] = jnp.concatenate([part[0:64, :], part[64:128, :]], axis=1).astype(bf16)

    def send_back(k):
        to = rem(me + k, N)
        pack_back(to)
        give_back.start_to(to)

    loop(1, N, send_back)
    pack_back(me)
    recv4[me] = send4[me]

    seq_first.wait_recv()
    for c in range(SPLIT // 128):
        value = add_up(seq_recv.at[:, :, 128 * c : 128 * c + 128])
        for b in range(N // 2):
            z_send2[b, 4 * c : 4 * c + 4, :] = value[4 * b : 4 * b + 4, :]
    z_second = Exchange(flights, *over_z, lambda to: z_send2.at[to], lambda s: z_recv2.at[s], z_sem2)
    z_second.start()
    z_recv2[z] = z_send2[z]

    z_first.wait_recv()
    for c in range((D - SPLIT) // 128):
        value = add_up(z_recv.at[:, :, 128 * c : 128 * c + 128])
        for j in range(N):
            seq_send2[j, 4 * c : 4 * c + 4, :] = value[4 * j : 4 * j + 4, :]
    seq_second = Exchange(flights, *over_seq, lambda to: seq_send2.at[to], lambda s: seq_recv2.at[s], seq_sem2)
    seq_second.start()
    seq_recv2[me] = seq_send2[me]

    ksum3.wait_recv()
    for c in range(D // 128):
        columns = slice(128 * c, 128 * c + 128)
        ktaps_ref[:, columns] = kall[32 * c : 32 * c + TAPS, :]
        ggain_ref[:, columns] = kall[32 * c + TAPS : 32 * c + 32, :]

    give_back.wait_recv()

    def unpack(j):
        a, b = recv4[2 * j], recv4[2 * j + 1]
        columns = pl.ds(times(j, 128), 128)
        dk_ref[:, columns] = jnp.concatenate([a[0:F, :64], b[0:F, :64]], axis=1)
        dv_ref[:, columns] = jnp.concatenate([a[0:F, 64:], b[0:F, 64:]], axis=1)
        dq_ref[0:64, columns] = jnp.concatenate([a[F:, :64], b[F:, :64]], axis=1)
        dq_ref[64:128, columns] = jnp.concatenate([a[F:, 64:], b[F:, 64:]], axis=1)

    loop(0, N // 2, unpack)
    for store in stores[2:]:
        store.start()

    z_second.wait_recv()
    value = add_up(z_recv2)
    for c in range(SPLIT // 128):
        wgrad_ref[:, 128 * c : 128 * c + 128] = value[4 * c : 4 * c + 4, :]
    seq_second.wait_recv()
    value = add_up(seq_recv2)
    for c in range((D - SPLIT) // 128):
        wgrad_ref[:, SPLIT + 128 * c : SPLIT + 128 * c + 128] = value[4 * c : 4 * c + 4, :]

    for store in stores:
        store.wait()
    for flight in flights:
        flight.wait_send()


def hand_over(*refs):
    sources, targets, held, sems = refs[:8], refs[8:16], refs[16:23], refs[23]
    loads = [pltpu.make_async_copy(sources[i], held[i], sems.at[0, i]) for i in range(7)]
    stores = [pltpu.make_async_copy(held[i], targets[i], sems.at[1, i]) for i in range(7)]
    for load in loads:
        load.start()
    targets[7][...] = sources[7][0, :]
    for load, store in zip(loads, stores):
        load.wait()
        store.start()
    for store in stores:
        store.wait()


def local(resid, query, key, value, out_weight, conv_kernel, conv_gain, recording_ids, cotangent):
    vmem = pl.BlockSpec(memory_space=pltpu.VMEM)
    hbm = pl.BlockSpec(memory_space=pl.ANY)
    scratch = [
        pltpu.VMEM((F, A), bf16),
        pltpu.VMEM((F, A), bf16),
        pltpu.VMEM((F, A), bf16),
        pltpu.VMEM((TAPS, D), f32),
        pltpu.VMEM((1, D), f32),
        pltpu.VMEM((F, D), bf16),
        pltpu.VMEM((F, A), bf16),
        pltpu.VMEM((F, A), bf16),
        pltpu.VMEM((F, A), bf16),
        pltpu.VMEM((8, 152, D), f32),
        pltpu.VMEM((8, 152, D), f32),
        pltpu.VMEM((N, F, 128), bf16),
        pltpu.VMEM((N, F, 128), bf16),
        pltpu.VMEM((N, 64, 128), bf16),
        pltpu.VMEM((N, 64, 128), bf16),
        pltpu.VMEM((N, 8, 128), i32),
        pltpu.VMEM((L + F, 128), f32),
        pltpu.VMEM((L + F, H), f32),
        pltpu.VMEM((L, H), bf16),
        pltpu.VMEM((L, H), bf16),
        pltpu.VMEM((L, H), bf16),
        pltpu.VMEM((L, BIG), bf16),
        pltpu.VMEM((L + F, H), f32),
        pltpu.VMEM((N, 64, 128), bf16),
        pltpu.VMEM((N, 64, 128), bf16),
        pltpu.VMEM((2, F, A), bf16),
        pltpu.VMEM((A, D), bf16),
        pltpu.VMEM((F, D), bf16),
        pltpu.VMEM((F, D), bf16),
        pltpu.VMEM((F, D), f32),
        pltpu.VMEM((F, D), f32),
        pltpu.VMEM((F + 2 * EDGE, D), f32),
        pltpu.VMEM((F + 2 * EDGE, D), f32),
        pltpu.VMEM((F, D), f32),
        pltpu.VMEM((F, D), bf16),
        pltpu.VMEM((F, 128), i32),
        pltpu.VMEM((F, 128), i32),
        pltpu.VMEM((F, 128), f32),
        pltpu.VMEM((4, EDGE, D), bf16),
        pltpu.VMEM((4, EDGE, D), bf16),
        pltpu.VMEM((N, 64, 128), bf16),
        pltpu.VMEM((N, 64, 128), bf16),
        pltpu.VMEM((N, 192, 128), bf16),
        pltpu.VMEM((N, 192, 128), bf16),
        pltpu.VMEM((L + F, H), f32),
        pltpu.VMEM((L, H), bf16),
        pltpu.VMEM((2 * H, L), f32),
        pltpu.VMEM((2, 32, SPLIT), f32),
        pltpu.VMEM((8, 64, D), f32),
        pltpu.VMEM((8, 64, D), bf16),
        pltpu.VMEM((8, 64, D), bf16),
        pltpu.VMEM((8, 64, D - SPLIT), bf16),
        pltpu.VMEM((8, 64, D - SPLIT), bf16),
        pltpu.VMEM((N, 32, SPLIT), bf16),
        pltpu.VMEM((N, 32, SPLIT), bf16),
        pltpu.VMEM((8, SPLIT // 32, 128), f32),
        pltpu.VMEM((8, SPLIT // 32, 128), f32),
        pltpu.VMEM((N, (D - SPLIT) // 32, 128), f32),
        pltpu.VMEM((N, (D - SPLIT) // 32, 128), f32),
        pltpu.VMEM((384, 128), f32),
        pltpu.VMEM((N, 24, 128), f32),
        pltpu.VMEM((24, 128), f32),
        pltpu.VMEM((N, 24, 128), f32),
        pltpu.VMEM((384, 128), f32),
        pltpu.SemaphoreType.DMA((12,)),
        pltpu.SemaphoreType.DMA((2, N)),
        pltpu.SemaphoreType.DMA((2, N)),
        pltpu.SemaphoreType.DMA((2, N)),
        pltpu.SemaphoreType.DMA((2, N)),
        pltpu.SemaphoreType.DMA((2, N)),
        pltpu.SemaphoreType.DMA((2, N)),
        pltpu.SemaphoreType.DMA((2, 4)),
        pltpu.SemaphoreType.DMA((2, 8)),
        pltpu.SemaphoreType.DMA((2, 8)),
        pltpu.SemaphoreType.DMA((2, N)),
        pltpu.SemaphoreType.DMA((2, 8)),
        pltpu.SemaphoreType.DMA((2, N)),
        pltpu.SemaphoreType.DMA((2, N)),
        pltpu.SemaphoreType.DMA((2, N)),
        pltpu.SemaphoreType.DMA((2, N)),
    ]
    outs = pl.pallas_call(
        kernel,
        out_shape=(
            jax.ShapeDtypeStruct((F, D), bf16),
            jax.ShapeDtypeStruct((F, D), bf16),
            jax.ShapeDtypeStruct((F, A), bf16),
            jax.ShapeDtypeStruct((F, A), bf16),
            jax.ShapeDtypeStruct((F, A), bf16),
            jax.ShapeDtypeStruct((4, D), f32),
            jax.ShapeDtypeStruct((TAPS, D), f32),
            jax.ShapeDtypeStruct((1, D), f32),
        ),
        in_specs=[hbm] * 3 + [vmem, hbm, vmem] + [hbm] * 3,
        out_specs=(hbm,) * 5 + (vmem,) * 3,
        scratch_shapes=scratch,
        compiler_params=pltpu.CompilerParams(
            collective_id=0, has_side_effects=True, vmem_limit_bytes=60 * 1024 * 1024
        ),
        name="conformer",
    )(
        query[0], key[0], value[0], recording_ids, conv_kernel, conv_gain,
        resid[0], cotangent[0], out_weight,
    )
    layer_out, grad_resid, grad_q, grad_k, grad_v, grad_w, grad_taps, grad_gain = pl.pallas_call(
        hand_over,
        out_shape=tuple(jax.ShapeDtypeStruct(out.shape, out.dtype) for out in outs[:7])
        + (jax.ShapeDtypeStruct((D,), f32),),
        in_specs=[hbm] * 7 + [vmem],
        out_specs=(hbm,) * 7 + (vmem,),
        scratch_shapes=[pltpu.VMEM(out.shape, out.dtype) for out in outs[:7]]
        + [pltpu.SemaphoreType.DMA((2, 7))],
        name="hand_over",
    )(*outs)
    return (
        layer_out[None], grad_resid[None], grad_q[None], grad_k[None], grad_v[None],
        grad_w, grad_taps, grad_gain,
    )


def solution(mesh):
    rows = P("dp", "seq", None)
    return jax.shard_map(
        local,
        mesh=mesh,
        in_specs=(rows, rows, rows, rows, P(), P(), P(), P("dp", "seq"), rows),
        out_specs=(rows, rows, rows, rows, rows, P(("dp", "seq"), None), P(), P()),
        check_vma=False,
    )
```

time: 130 us -> 102 us (0.78); the launches traced: 129 us -> 99.8 us
  Pallas kernels: 116 us -> 99.2 us
  local copies, waits for them, and re-layouts: 11.1 us -> 0 us
  other arithmetic: 1.35 us -> 0 us
    pallas_call x1, Pallas kernels: 116 us -> 95.6 us  [local(): pl.pallas_call(kernel, out_shape=(jax.ShapeDtypeStruct((F, D), bf16), jax...]
    unnamed x11 -> x0, local copies, waits for them, and re-layouts: 9.83 us -> none
    pallas_call x0 -> x1, Pallas kernels: none -> 3.61 us  [local(): pl.pallas_call(hand_over, out_shape=tuple((jax.ShapeDtypeStruct(out.shape...]
    pallas_call x1 -> x0, other arithmetic: 1.35 us -> none  [local(): pl.pallas_call(kernel, out_shape=(jax.ShapeDtypeStruct((F, D), bf16), jax...]
where the time goes in v2:
time: 102 us; the launch traced here: 99.8 us
  Pallas kernels  99.2 us (97%)
    pallas_call x1, Pallas kernels, local(): pl.pallas_call(kernel, out_shape=(jax.ShapeDtypeStruct((F, D), bf16), jax...  95.6 us
    pallas_call x1, Pallas kernels, local(): pl.pallas_call(hand_over, out_shape=tuple((jax.ShapeDtypeStruct(out.shape...  3.61 us

profile of v2, /device:TPU:8, one launch (start us, length us, event | category | flops | bytes accessed | tf_op | source)
XLA Modules:
  0.0 99.8 jit_solution(14663409693811767876)
XLA Ops:
  0.6 95.6 %conformer.1 = (bf16[128,1536]{1,0:T(8,128)(2,1)}, bf16[128,1536]{1,0:T(8,128)(2,1)}, bf16[128,1024]{1,0:T(8,128)(2,1)}, bf16[128,1024]{1,0:T(8,128)(2,1)}, bf16...) custom-call(bf16[128,1024]{1,0:T(8,128)(2,1)} %bitcast.12, ...), custom_call_target="tpu_custom_call" | custom-call | tf_op jit(solution)/shard_map/conformer/pallas_call | solution.py:717
  96.2 3.6 %hand_over.1 = (bf16[128,1536]{1,0:T(8,128)(2,1)}, bf16[128,1536]{1,0:T(8,128)(2,1)}, bf16[128,1024]{1,0:T(8,128)(2,1)}, bf16[128,1024]{1,0:T(8,128)(2,1)}, bf16...) custom-call(bf16[128,1536]{1,0:T(8,128)(2,1)} %get-tuple-element.24.refs_0_, ...), custom_call_target="tpu_custom_call" | custom-call | tf_op jit(solution)/shard_map/hand_over/pallas_call | solution.py:740

commit v3 on v2

--- a/solution.py
+++ b/solution.py
@@ -98,10 +98,10 @@
 
 def kernel(
     q_hbm, k_hbm, v_hbm, ids_ref, taps_hbm, gain_in, resid_hbm, cot_hbm, w_hbm,
-    layer_hbm, gresid_hbm, dq_hbm, dk_hbm, dv_hbm, wgrad_ref, ktaps_ref, ggain_ref,
-    q_ref, k_ref, v_ref, taps_ref, gain_ref, layer_ref, dq_ref, dk_ref, dv_ref, shift, gshift, send0, recv0,
+    layer_ref, gres, dq_ref, dk_ref, dv_ref, wgrad_ref, ktaps_ref, ggain_ref,
+    q_ref, k_ref, v_ref, taps_ref, gain_ref, shift, gshift, send0, recv0,
     send1, recv1, ids_all, rot_qk, rot_v, qr, kr, vr, probs, out_rot, send2, recv2, attn,
-    w_ref, resid_ref, cot_ref, stream, normed, pad, gpad, gshaped, gres, near_next, near_prev, dots_ref,
+    w_ref, resid_ref, cot_ref, stream, normed, pad, gpad, gshaped, near_next, near_prev, dots_ref,
     edge_send, edge_recv, send3, recv3, send4, recv4, rot_g, gr, kv_acc,
     two, own, core_send, core_recv, z_send, z_recv, seq_send, seq_recv, z_send2, z_recv2, seq_send2, seq_recv2,
     kpart, krecv, ksum, krecv2, kall,
@@ -116,11 +116,10 @@
     pairs = (
         (q_hbm, q_ref), (k_hbm, k_ref), (v_hbm, v_ref),
         (w_hbm, w_ref), (resid_hbm, resid_ref), (cot_hbm, cot_ref), (taps_hbm, taps_ref),
-        (layer_ref, layer_hbm), (gres, gresid_hbm), (dq_ref, dq_hbm), (dk_ref, dk_hbm), (dv_ref, dv_hbm),
     )
     moves = [pltpu.make_async_copy(a, b, local_sem.at[i]) for i, (a, b) in enumerate(pairs)]
-    first, loads, stores = moves[:3], moves[3:7], moves[7:]
-    for load in first + loads:
+    first, loads = moves[:3], moves[3:]
+    for load in first:
         load.start()
     gain_ref[0, :] = gain_in[...]
 
@@ -134,6 +133,8 @@
 
     for load in first:
         load.wait()
+    for load in loads:
+        load.start()
 
     def pack_qkv(j):
         columns = pl.ds(times(j, 128), 128)
@@ -197,7 +198,7 @@
         column_part = column_part + jnp.where(column >= mark, 1, 0)
 
     def weigh(base, masked):
-        def tile(t):
+        def one(t):
             rows = pl.ds(pl.multiple_of(base + t * TILE, TILE), TILE)
             scores = dot(qr[rows, :], kr[base : base + BIG, :], NT)
             if masked:
@@ -209,7 +210,11 @@
             unnormed = jnp.exp(scores - jnp.max(scores, axis=1, keepdims=True))
             probs[rows, :] = (unnormed * (1.0 / jnp.sum(unnormed, axis=1, keepdims=True))).astype(bf16)
 
-        loop(0, BIG // TILE, tile)
+        def two_tiles(t):
+            one(2 * t)
+            one(2 * t + 1)
+
+        loop(0, BIG // TILE // 2, two_tiles)
 
     weigh(0, False)
     weigh(BIG, True)
@@ -334,7 +339,7 @@
                 sums[k] = sums[k] + (jnp.where(mask, part, 0.0) if step else part)
         return sums
 
-    WIDE, TALL = 2, 64
+    WIDE, TALL, EARLY = 2, 64, 2
 
     def convolve(low, tall):
         rows = slice(low, low + tall)
@@ -368,7 +373,6 @@
     grad_halo = edges(1)
     grad_halo.start(0)
     grad_halo.start(1)
-    stores[0].start()
 
     shift_rows(gpad, gshift, 16, 128)
 
@@ -383,7 +387,7 @@
                     part = jnp.where(mask, part, 0.0)
                 kpart[pl.ds((c * WIDE + k) * 32 + i, 1), :] = jnp.sum(part, axis=0, keepdims=True)
 
-    loop(0, D // (128 * WIDE), kernel_rows)
+    loop(0, EARLY, kernel_rows)
     grad_halo.wait_recv()
     gpad[EDGE + F :, :] = edge_recv[2].astype(f32)
     gpad[0:EDGE, :] = edge_recv[3].astype(f32)
@@ -410,12 +414,6 @@
     loop(0, D // (128 * WIDE), convolve_back)
     mean = jnp.sum(dots_ref[...], axis=1, keepdims=True) * (1.0 / D)
 
-    def kpiece(s):
-        return pl.ds(pl.multiple_of(s * 24, 8), 24)
-
-    ksum1 = Exchange(flights, *over_seq, lambda to: kpart.at[kpiece(to)], lambda s: krecv.at[s], ksem1)
-    ksum1.start()
-
     def into_stream(c):
         columns = pl.ds(times(c, 256), 256)
         part = gshaped[:, columns] - normed[:, columns] * mean
@@ -423,7 +421,6 @@
         gres[:, columns] = grad
 
     loop(0, D // 256, into_stream)
-    stores[1].start()
 
     give_grad = Exchange(flights, *over_seq, lambda to: send3.at[to], lambda s: recv3.at[s], sem3)
 
@@ -460,6 +457,14 @@
 
     loop(0, N // 2, project_grad)
 
+    loop(EARLY, D // (128 * WIDE), kernel_rows)
+
+    def kpiece(s):
+        return pl.ds(pl.multiple_of(s * 24, 8), 24)
+
+    ksum1 = Exchange(flights, *over_seq, lambda to: kpart.at[kpiece(to)], lambda s: krecv.at[s], ksem1)
+    ksum1.start()
+
     give_grad.wait_recv()
 
     def widen_grad(i):
@@ -474,9 +479,6 @@
         gr[pl.ds(times(i, F), F), :] = rot_g[pl.ds((start + i * F) & (L - 1), F), :].astype(bf16)
 
     loop(0, N, turn_grad)
-
-    ksum1.wait_recv()
-    krecv[me] = kpart[kpiece(me), :]
 
     def add_up(ref):
         value = ref[0].astype(f32)
@@ -484,10 +486,6 @@
             value = value + ref[i].astype(f32)
         return value
 
-    ksum[...] = add_up(krecv)
-    ksum2 = Exchange(flights, *over_dp, lambda to: ksum, lambda s: krecv2.at[s], ksem2)
-    ksum2.start()
-    krecv2[dp] = ksum[...]
     to_core.wait_recv()
 
     z_first = Exchange(flights, *over_z, lambda to: z_send.at[to], lambda s: z_recv.at[s], z_sem)
@@ -533,10 +531,13 @@
 
     loop(0, L // TILE, back)
 
-    ksum2.wait_recv()
-    kall[kpiece(me), :] = add_up(krecv2)
-    ksum3 = Exchange(flights, *over_seq, lambda to: kall.at[kpiece(me)], lambda s: kall.at[kpiece(s)], ksem3)
-    ksum3.start()
+    ksum1.wait_recv()
+    krecv[me] = kpart[kpiece(me), :]
+
+    ksum[...] = add_up(krecv)
+    ksum2 = Exchange(flights, *over_dp, lambda to: ksum, lambda s: krecv2.at[s], ksem2)
+    ksum2.start()
+    krecv2[dp] = ksum[...]
 
     def upright(i):
         rows = pl.ds(times(i, F), F)
@@ -571,6 +572,11 @@
     z_second.start()
     z_recv2[z] = z_send2[z]
 
+    ksum2.wait_recv()
+    kall[kpiece(me), :] = add_up(krecv2)
+    ksum3 = Exchange(flights, *over_seq, lambda to: kall.at[kpiece(me)], lambda s: kall.at[kpiece(s)], ksem3)
+    ksum3.start()
+
     z_first.wait_recv()
     for c in range((D - SPLIT) // 128):
         value = add_up(z_recv.at[:, :, 128 * c : 128 * c + 128])
@@ -597,8 +603,6 @@
         dq_ref[64:128, columns] = jnp.concatenate([a[F:, 64:], b[F:, 64:]], axis=1)
 
     loop(0, N // 2, unpack)
-    for store in stores[2:]:
-        store.start()
 
     z_second.wait_recv()
     value = add_up(z_recv2)
@@ -609,24 +613,18 @@
     for c in range((D - SPLIT) // 128):
         wgrad_ref[:, SPLIT + 128 * c : SPLIT + 128 * c + 128] = value[4 * c : 4 * c + 4, :]
 
-    for store in stores:
-        store.wait()
     for flight in flights:
         flight.wait_send()
 
 
 def hand_over(*refs):
-    sources, targets, held, sems = refs[:8], refs[8:16], refs[16:23], refs[23]
-    loads = [pltpu.make_async_copy(sources[i], held[i], sems.at[0, i]) for i in range(7)]
-    stores = [pltpu.make_async_copy(held[i], targets[i], sems.at[1, i]) for i in range(7)]
-    for load in loads:
-        load.start()
+    sources, targets, sems = refs[:8], refs[8:16], refs[16]
+    copies = [pltpu.make_async_copy(sources[i], targets[i], sems.at[i]) for i in range(7)]
+    for copy in copies:
+        copy.start()
     targets[7][...] = sources[7][0, :]
-    for load, store in zip(loads, stores):
-        load.wait()
-        store.start()
-    for store in stores:
-        store.wait()
+    for copy in copies:
+        copy.wait()
 
 
 def local(resid, query, key, value, out_weight, conv_kernel, conv_gain, recording_ids, cotangent):
@@ -638,10 +636,6 @@
         pltpu.VMEM((F, A), bf16),
         pltpu.VMEM((TAPS, D), f32),
         pltpu.VMEM((1, D), f32),
-        pltpu.VMEM((F, D), bf16),
-        pltpu.VMEM((F, A), bf16),
-        pltpu.VMEM((F, A), bf16),
-        pltpu.VMEM((F, A), bf16),
         pltpu.VMEM((8, 152, D), f32),
         pltpu.VMEM((8, 152, D), f32),
         pltpu.VMEM((N, F, 128), bf16),
@@ -667,7 +661,6 @@
         pltpu.VMEM((F + 2 * EDGE, D), f32),
         pltpu.VMEM((F + 2 * EDGE, D), f32),
         pltpu.VMEM((F, D), f32),
-        pltpu.VMEM((F, D), bf16),
         pltpu.VMEM((F, 128), i32),
         pltpu.VMEM((F, 128), i32),
         pltpu.VMEM((F, 128), f32),
@@ -697,7 +690,7 @@
         pltpu.VMEM((24, 128), f32),
         pltpu.VMEM((N, 24, 128), f32),
         pltpu.VMEM((384, 128), f32),
-        pltpu.SemaphoreType.DMA((12,)),
+        pltpu.SemaphoreType.DMA((7,)),
         pltpu.SemaphoreType.DMA((2, N)),
         pltpu.SemaphoreType.DMA((2, N)),
         pltpu.SemaphoreType.DMA((2, N)),
@@ -717,17 +710,17 @@
     outs = pl.pallas_call(
         kernel,
         out_shape=(
-            jax.ShapeDtypeStruct((F, D), bf16),
-            jax.ShapeDtypeStruct((F, D), bf16),
-            jax.ShapeDtypeStruct((F, A), bf16),
-            jax.ShapeDtypeStruct((F, A), bf16),
-            jax.ShapeDtypeStruct((F, A), bf16),
-            jax.ShapeDtypeStruct((4, D), f32),
-            jax.ShapeDtypeStruct((TAPS, D), f32),
-            jax.ShapeDtypeStruct((1, D), f32),
+            pltpu.VMEM((F, D), bf16),
+            pltpu.VMEM((F, D), bf16),
+            pltpu.VMEM((F, A), bf16),
+            pltpu.VMEM((F, A), bf16),
+            pltpu.VMEM((F, A), bf16),
+            pltpu.VMEM((4, D), f32),
+            pltpu.VMEM((TAPS, D), f32),
+            pltpu.VMEM((1, D), f32),
         ),
         in_specs=[hbm] * 3 + [vmem, hbm, vmem] + [hbm] * 3,
-        out_specs=(hbm,) * 5 + (vmem,) * 3,
+        out_specs=(vmem,) * 8,
         scratch_shapes=scratch,
         compiler_params=pltpu.CompilerParams(
             collective_id=0, has_side_effects=True, vmem_limit_bytes=60 * 1024 * 1024
@@ -741,12 +734,11 @@
         hand_over,
         out_shape=tuple(jax.ShapeDtypeStruct(out.shape, out.dtype) for out in outs[:7])
         + (jax.ShapeDtypeStruct((D,), f32),),
-        in_specs=[hbm] * 7 + [vmem],
+        in_specs=[vmem] * 8,
         out_specs=(hbm,) * 7 + (vmem,),
-        scratch_shapes=[pltpu.VMEM(out.shape, out.dtype) for out in outs[:7]]
-        + [pltpu.SemaphoreType.DMA((2, 7))],
+        scratch_shapes=[pltpu.SemaphoreType.DMA((7,))],
         name="hand_over",
-    )(*outs)
+    )(*(pltpu.with_memory_space_constraint(out, pltpu.VMEM) for out in outs))
     return (
         layer_out[None], grad_resid[None], grad_q[None], grad_k[None], grad_v[None],
         grad_w, grad_taps, grad_gain,

time: 102 us -> 96.2 us (0.943); the launches traced: 99.8 us -> 96 us
  Pallas kernels: 99.2 us -> 95.4 us
    pallas_call x1, Pallas kernels: 95.6 us -> 93.5 us  [local(): pl.pallas_call(kernel, out_shape=(pltpu.VMEM((F, D), bf16), pltpu.VMEM((F...]
    pallas_call x1, Pallas kernels: 3.61 us -> 1.86 us  [local(): pl.pallas_call(hand_over, out_shape=tuple((jax.ShapeDtypeStruct(out.shape...]
where the time goes in v3:
time: 96.2 us; the launch traced here: 96 us
  Pallas kernels  95.4 us (99%)
    pallas_call x1, Pallas kernels, local(): pl.pallas_call(kernel, out_shape=(pltpu.VMEM((F, D), bf16), pltpu.VMEM((F...  93.5 us

profile of v3, /device:TPU:8, one launch (start us, length us, event | category | flops | bytes accessed | tf_op | source)
XLA Modules:
  0.0 96.0 jit_solution(13658010615150642354)
XLA Ops:
  0.6 93.5 %conformer.1 = (bf16[128,1536]{1,0:T(8,128)(2,1)S(1)}, bf16[128,1536]{1,0:T(8,128)(2,1)S(1)}, bf16[128,1024]{1,0:T(8,128)(2,1)S(1)}, bf16[128,1024]{1,0:T(8,128)...) custom-call(bf16[128,1024]{1,0:T(8,128)(2,1)} %bitcast.12, ...), custom_call_target="tpu_custom_call" | custom-call | tf_op jit(solution)/shard_map/conformer/pallas_call | solution.py:710
  94.2 1.9 %hand_over.1 = (bf16[128,1536]{1,0:T(8,128)(2,1)}, bf16[128,1536]{1,0:T(8,128)(2,1)}, bf16[128,1024]{1,0:T(8,128)(2,1)}, bf16[128,1024]{1,0:T(8,128)(2,1)}, bf16...) custom-call(bf16[128,1536]{1,0:T(8,128)(2,1)S(1)} %get-tuple-element.24.refs_0_, ...), custom_call_target="tpu_custom_call" | custom-call | tf_op jit(solution)/shard_map/hand_over/pallas_call | solution.py:733

commit v4 on v3

--- a/solution.py
+++ b/solution.py
@@ -239,7 +239,7 @@
         keys = pl.ds(times(t // (BIG // TILE), BIG), BIG)
         out_rot[rows, :] = dot(probs[rows, :], vr[keys, :], NN).astype(bf16).astype(f32)
 
-    loop(0, L // TILE, mix)
+    loop(0, L // TILE // 2, lambda t: (mix(2 * t), mix(2 * t + 1)))
     out_rot[L : L + F, :] = out_rot[0:F, :]
 
     give_out = Exchange(flights, *over_seq, lambda to: send2.at[to], lambda s: recv2.at[s], sem2)
@@ -339,7 +339,7 @@
                 sums[k] = sums[k] + (jnp.where(mask, part, 0.0) if step else part)
         return sums
 
-    WIDE, TALL, EARLY = 2, 64, 2
+    WIDE, TALL, EARLY = 2, 32, 2
 
     def convolve(low, tall):
         rows = slice(low, low + tall)
@@ -361,7 +361,8 @@
 
         loop(0, D // (128 * WIDE), one)
 
-    convolve(32, 64)
+    convolve(32, 32)
+    convolve(64, 32)
     halo.wait_recv()
     pad[EDGE + F :, :] = edge_recv[0].astype(f32)
     pad[0:EDGE, :] = edge_recv[1].astype(f32)
@@ -529,7 +530,7 @@
         kv_acc[0:H, keys] += dot(qr[rows, :], slope, TN)
         kv_acc[H:, keys] += dot(grad, weights, TN)
 
-    loop(0, L // TILE, back)
+    loop(0, L // TILE // 2, lambda t: (back(2 * t), back(2 * t + 1)))
 
     ksum1.wait_recv()
     krecv[me] = kpart[kpiece(me), :]

time: 96.2 us -> 94.9 us (0.986)
  Pallas kernels: 95.4 us -> 94.1 us
    pallas_call x1, Pallas kernels: 93.5 us -> 92.2 us  [local(): pl.pallas_call(kernel, out_shape=(pltpu.VMEM((F, D), bf16), pltpu.VMEM((F...]
where the time goes in v4:
time: 94.9 us; the launch traced here: 94.7 us
  Pallas kernels  94.1 us (99%)
    pallas_call x1, Pallas kernels, local(): pl.pallas_call(kernel, out_shape=(pltpu.VMEM((F, D), bf16), pltpu.VMEM((F...  92.2 us

profile of v4, /device:TPU:8, one launch (start us, length us, event | category | flops | bytes accessed | tf_op | source)
XLA Modules:
  0.0 94.7 jit_solution(17175955547195636969)
XLA Ops:
  0.6 92.2 %conformer.1 = (bf16[128,1536]{1,0:T(8,128)(2,1)S(1)}, bf16[128,1536]{1,0:T(8,128)(2,1)S(1)}, bf16[128,1024]{1,0:T(8,128)(2,1)S(1)}, bf16[128,1024]{1,0:T(8,128)...) custom-call(bf16[128,1024]{1,0:T(8,128)(2,1)} %bitcast.12, ...), custom_call_target="tpu_custom_call" | custom-call | tf_op jit(solution)/shard_map/conformer/pallas_call | solution.py:711
  92.9 1.9 %hand_over.1 = (bf16[128,1536]{1,0:T(8,128)(2,1)}, bf16[128,1536]{1,0:T(8,128)(2,1)}, bf16[128,1024]{1,0:T(8,128)(2,1)}, bf16[128,1024]{1,0:T(8,128)(2,1)}, bf16...) custom-call(bf16[128,1536]{1,0:T(8,128)(2,1)S(1)} %get-tuple-element.24.refs_0_, ...), custom_call_target="tpu_custom_call" | custom-call | tf_op jit(solution)/shard_map/hand_over/pallas_call | solution.py:734

commit v5 on v4

--- a/solution.py
+++ b/solution.py
@@ -35,6 +35,10 @@
 
 def times(value, size):
     return pl.multiple_of(value * size, size)
+
+
+def loop_by_four(count, body):
+    loop(0, count // 4, lambda i: [body(4 * i + k) for k in range(4)])
 
 
 def dot(a, b, dims):
@@ -181,7 +185,7 @@
     def widen(i):
         rot_qk[pl.ds(times(i, F), F), :] = recv0[i].astype(f32)
 
-    loop(0, N, widen)
+    loop_by_four(N, widen)
     rot_qk[L : L + F, :] = rot_qk[0:F, :]
 
     def turn(i):
@@ -190,7 +194,7 @@
         qr[rows, :] = (both[:, :64] * H**-0.5).astype(bf16)
         kr[rows, :] = both[:, 64:].astype(bf16)
 
-    loop(0, N, turn)
+    loop_by_four(N, turn)
 
     column = lax.broadcasted_iota(i32, (1, BIG), 1)
     column_part = jnp.zeros((1, BIG), i32)
@@ -226,13 +230,13 @@
         rot_v[pl.ds(times(i, F), 64), :] = values[:, :64]
         rot_v[pl.ds(pl.multiple_of(i * F + 64, 64), 64), :] = values[:, 64:]
 
-    loop(0, N, widen_v)
+    loop_by_four(N, widen_v)
     rot_v[L : L + F, :] = rot_v[0:F, :]
 
     def turn_v(i):
         vr[pl.ds(times(i, F), F), :] = rot_v[pl.ds((start + i * F) & (L - 1), F), :].astype(bf16)
 
-    loop(0, N, turn_v)
+    loop_by_four(N, turn_v)
 
     def mix(t):
         rows = pl.ds(times(t, TILE), TILE)
@@ -473,13 +477,13 @@
         rot_g[pl.ds(times(i, F), 64), :] = values[:, :64]
         rot_g[pl.ds(pl.multiple_of(i * F + 64, 64), 64), :] = values[:, 64:]
 
-    loop(0, N, widen_grad)
+    loop_by_four(N, widen_grad)
     rot_g[L : L + F, :] = rot_g[0:F, :]
 
     def turn_grad(i):
         gr[pl.ds(times(i, F), F), :] = rot_g[pl.ds((start + i * F) & (L - 1), F), :].astype(bf16)
 
-    loop(0, N, turn_grad)
+    loop_by_four(N, turn_grad)
 
     def add_up(ref):
         value = ref[0].astype(f32)
@@ -544,7 +548,7 @@
         rows = pl.ds(times(i, F), F)
         rot_qk[rows, :] = kv_acc[:, rows].T
 
-    loop(0, N, upright)
+    loop_by_four(N, upright)
     rot_qk[L : L + F, :] = rot_qk[0:F, :]
     rot_v[L : L + F, :] = rot_v[0:F, :]
     give_back = Exchange(flights, *over_seq, lambda to: send4.at[to], lambda s: recv4.at[s], sem4)

time: 94.9 us -> 92.2 us (0.972)
  Pallas kernels: 94.1 us -> 91.5 us
    pallas_call x1, Pallas kernels: 92.2 us -> 89.6 us  [local(): pl.pallas_call(kernel, out_shape=(pltpu.VMEM((F, D), bf16), pltpu.VMEM((F...]
where the time goes in v5:
time: 92.2 us; the launch traced here: 92.1 us
  Pallas kernels  91.5 us (99%)
    pallas_call x1, Pallas kernels, local(): pl.pallas_call(kernel, out_shape=(pltpu.VMEM((F, D), bf16), pltpu.VMEM((F...  89.6 us
    pallas_call x1, Pallas kernels, local(): pl.pallas_call(hand_over, out_shape=tuple((jax.ShapeDtypeStruct(out.shape...  1.86 us

profile of v5, /device:TPU:8, one launch (start us, length us, event | category | flops | bytes accessed | tf_op | source)
XLA Modules:
  0.0 92.1 jit_solution(7977785738697284389)
XLA Ops:
  0.6 89.6 %conformer.1 = (bf16[128,1536]{1,0:T(8,128)(2,1)S(1)}, bf16[128,1536]{1,0:T(8,128)(2,1)S(1)}, bf16[128,1024]{1,0:T(8,128)(2,1)S(1)}, bf16[128,1024]{1,0:T(8,128)...) custom-call(bf16[128,1024]{1,0:T(8,128)(2,1)} %bitcast.12, ...), custom_call_target="tpu_custom_call" | custom-call | tf_op jit(solution)/shard_map/conformer/pallas_call | solution.py:715
  90.2 1.9 %hand_over.1 = (bf16[128,1536]{1,0:T(8,128)(2,1)}, bf16[128,1536]{1,0:T(8,128)(2,1)}, bf16[128,1024]{1,0:T(8,128)(2,1)}, bf16[128,1024]{1,0:T(8,128)(2,1)}, bf16...) custom-call(bf16[128,1536]{1,0:T(8,128)(2,1)S(1)} %get-tuple-element.24.refs_0_, ...), custom_call_target="tpu_custom_call" | custom-call | tf_op jit(solution)/shard_map/hand_over/pallas_call | solution.py:738
